TPU v7x, 128 devices: a whole 4x4x4 slice. The times are simulated.
128 devices in a mesh: row: 8 (over z, y_hi), col: 16 (over y_lo, x, core).
Axes of the slice: x: 4, y: 4 (y_hi: 2, y_lo: 2; y = y_hi * 2 + y_lo), z: 4, core: 2. Of those that a mesh axis runs over, the one named last changes fastest.
Arguments:
- front: bfloat16 [16, 8, 128, 8, 16, 128], P(None, 'row', None, None, 'col'), may hold values from -8 to 25, as said below
- child_tiles: bfloat16 [16384, 128, 128], P(('row', 'col')), may hold values from -6 to 6
- tile_map: int32 [16384, 2], P(('row', 'col')), may hold values from 0 to 127, as said below
Outputs:
- factored: float32 [16, 8, 128, 8, 16, 128], P(None, 'row', None, None, 'col')
Inputs may be any that keep to these rules, and one draw needn't show every extreme that they name: The leading 2048 x 2048 block of front is symmetric positive definite. `tile_map`: each row names a parent row tile outside the first 16 row tiles; column tiles may be any, the panel's included. The owner of tile (i, j) is the device at row i % 8 and column j % 16; the 128 tiles of one device send at most 2 tiles to any one owner, and in every draw some owner receives 2 tiles from every device.
All inputs are finite; a program needn't handle non-finite values.
Results may differ from a plain program's by a relative error of at most 0.0013.
Values may be sent and summed in bfloat16 or wider, within the bound.
No kernel may reach another device: no remote copies, remote signals or barrier semaphores. Data moves between devices by JAX's collectives and lax.ppermute only.
A program may use at most 384 MiB of HBM per device.

v0:
```python
import jax
import jax.numpy as jnp
from jax import lax
from jax.sharding import PartitionSpec as P

PANEL = 2048
CAP = 2


def spread(block, axis, source):
    block = jnp.where(lax.axis_index(axis) == source, block, jnp.zeros_like(block))
    return lax.psum(block, axis)


def per_device(front, child_tiles, tile_map):
    rows_local = front.shape[0]
    tile_size = front.shape[2]
    cols_local = front.shape[3]
    row_count = lax.axis_size("row")
    col_count = lax.axis_size("col")
    device_count = row_count * col_count
    row_index = lax.axis_index("row")
    col_index = lax.axis_index("col")
    panel_tiles = PANEL // tile_size
    corner_rows = panel_tiles // row_count
    corner_cols = panel_tiles // col_count
    owners = tile_map[:, 0] % row_count * col_count + tile_map[:, 1] % col_count
    local_ids = tile_map[:, 0] // row_count * cols_local + tile_map[:, 1] // col_count
    owner_hits = (owners[:, None] == jnp.arange(device_count)[None, :]).astype(jnp.int32)
    slot_rank = jnp.sum(jnp.cumsum(owner_hits, 0) * owner_hits, 1) - 1
    slot_index = owners * CAP + slot_rank
    packed = (
        jnp.zeros((device_count * CAP, tile_size, tile_size), jnp.bfloat16)
        .at[slot_index]
        .set(child_tiles)
    )
    targets = jnp.full((device_count * CAP,), -1, jnp.int32).at[slot_index].set(local_ids)
    arrived, arrived_ids = (
        lax.all_to_all(
            packed.reshape(device_count, CAP, tile_size, tile_size),
            ("row", "col"),
            split_axis=0,
            concat_axis=0,
            tiled=True,
        ),
        lax.all_to_all(
            targets.reshape(device_count, CAP),
            ("row", "col"),
            split_axis=0,
            concat_axis=0,
            tiled=True,
        ),
    )
    flat_tiles = arrived.reshape(device_count * CAP, tile_size * tile_size)
    flat_ids = arrived_ids.reshape(device_count * CAP)
    selector = (flat_ids[None, :] == jnp.arange(rows_local * cols_local)[:, None]).astype(
        jnp.bfloat16
    )
    added = jnp.dot(selector, flat_tiles, preferred_element_type=jnp.float32)
    added = added.reshape(rows_local, cols_local, tile_size, tile_size).transpose(0, 2, 1, 3)
    assembled = (
        front.reshape(rows_local, tile_size, cols_local, tile_size).astype(jnp.float32) + added
    ).astype(jnp.bfloat16)
    corner = assembled[:corner_rows, :, :corner_cols, :].reshape(
        corner_rows, 1, tile_size, corner_cols, 1, tile_size
    )
    corner = lax.all_gather(corner, "row", axis=1, tiled=True)
    corner = lax.all_gather(corner, "col", axis=4, tiled=True)
    lower_factor = jnp.linalg.cholesky(corner.reshape(PANEL, PANEL).astype(jnp.float32))
    panel_part = assembled[:, :, :corner_cols, :].reshape(
        rows_local, tile_size, corner_cols, 1, tile_size
    )
    share_tiles = rows_local // col_count
    mine = lax.all_to_all(panel_part, "col", split_axis=0, concat_axis=3, tiled=True)
    solved = lax.linalg.triangular_solve(
        lower_factor,
        mine.reshape(share_tiles * tile_size, PANEL).astype(jnp.float32),
        left_side=False,
        lower=True,
        transpose_a=True,
    )
    first_tile = col_index * share_tiles
    global_rows = ((first_tile + jnp.arange(share_tiles)) * row_count + row_index)[
        :, None
    ] * tile_size + jnp.arange(tile_size)[None, :]
    global_rows = global_rows.reshape(-1)
    known = lower_factor[jnp.minimum(global_rows, PANEL - 1)]
    solved_part = jnp.where((global_rows < PANEL)[:, None], known, solved).astype(jnp.bfloat16)
    row_panel = lax.all_gather(
        solved_part.reshape(share_tiles, tile_size, PANEL), "col", axis=0, tiled=True
    )
    row_panel = row_panel.reshape(rows_local * tile_size, PANEL)
    group_size = col_count // row_count
    picked = row_panel.reshape(cols_local, group_size, tile_size, PANEL)
    picked = lax.dynamic_index_in_dim(picked, col_index // row_count, 1, keepdims=False)
    col_panel = spread(picked, "row", col_index % row_count).reshape(cols_local * tile_size, PANEL)
    lower_rows = row_panel[corner_rows * tile_size :]
    right_cols = col_panel[corner_cols * tile_size :]
    update = lax.dot_general(
        lower_rows, right_cols, (((1,), (1,)), ((), ())), preferred_element_type=jnp.float32
    )
    trailing = assembled[corner_rows:, :, corner_cols:, :].astype(jnp.float32)
    trailing = trailing - update.reshape(
        rows_local - corner_rows, tile_size, cols_local - corner_cols, tile_size
    )
    panel_values = lax.dynamic_index_in_dim(
        row_panel.reshape(rows_local, tile_size, corner_cols, col_count, tile_size),
        col_index,
        3,
        keepdims=False,
    ).astype(jnp.float32)
    upper_zero = jnp.zeros(
        (corner_rows, tile_size, cols_local - corner_cols, tile_size), jnp.float32
    )
    right_part = jnp.concatenate([upper_zero, trailing], 0)
    result = jnp.concatenate([panel_values, right_part], 2)
    return result.reshape(rows_local, 1, tile_size, cols_local, 1, tile_size)


def solution(mesh):
    in_specs = (
        P(None, "row", None, None, "col", None),
        P(("row", "col"), None, None),
        P(("row", "col"), None),
    )
    out_specs = P(None, "row", None, None, "col", None)
    return jax.shard_map(
        per_device, mesh=mesh, in_specs=in_specs, out_specs=out_specs, check_vma=False
    )
```

profile of v0, /device:TPU:1, one launch (start us, length us, event | category | flops | bytes accessed | tf_op | source)
XLA Modules:
  0.0 1395.0 jit_solution(7873273509780611019)
XLA Ops:
  28.1 19.3 %scatter_fusion = bf16[256,128,128]{2,1,0:T(8,128)(2,1)} fusion(bf16[256,128,128]{2,1,0:T(8,128)(2,1)} %broadcast_in_dim.15, s32[128]{0:T(128)S(1)} %get-tuple-element.212, bf16[128,128,128]{2,1,0:T(8,128)(2,1)} %param.4), kind=kCustom, calls=%fused_computation.2 | custom fusion | bytes 12583424 | tf_op jit(solution)/shard_map/scatter | solution.py:35
  59.5 96.8 %all-to-all-done.1 = bf16[128,2,128,128]{3,2,1,0:T(8,128)(2,1)} async-done(((bf16[128,2,128,128]{3,2,1,0:T(8,128)(2,1)}), bf16[128,2,128,128]{3,2,1,0:T(8,128)(2,1)}, u32[]{:S(2)}, u32[]{:S(2)}) %all-to-all-start.1) | async-done | bytes 8388640 | tf_op jit(solution)/shard_map/all_to_all | solution.py:39
  156.2 23.3 %copy.64 = bf16[32,8,128,128]{3,1,2,0:T(8,128)(2,1)} copy(bf16[32,8,128,128]{3,2,1,0:T(8,128)(2,1)} %bitcast.111) | data formatting | bytes 16777216
  179.5 11.9 copy.40
  201.0 32.8 %all-gather = bf16[2,1024,1,128]{3,2,1,0:T(2,128)(2,1)S(1)} all-gather(bf16[2,128,1,128]{3,2,1,0:T(2,128)(2,1)S(1)} %slice.508), channel_id=2, replica_groups=mesh['row'=8,'col'=16] {'row'}, dimensions={1}, use_global_device_ids=true | all-gather | bytes 589824 | tf_op jit(solution)/shard_map/all_gather | solution.py:67
  238.7 13.8 all-to-all-start.2
  252.6 14.2 %all-to-all-done.2 = bf16[16,128,1,1,128]{4,1,3,2,0:T(8,128)(2,1)S(1)} async-done(((bf16[16,128,1,1,128]{4,1,3,2,0:T(8,128)(2,1)}), bf16[16,128,1,1,128]{4,1,3,2,0:T(8,128)(2,1)S(1)}, u32[]{:S(2)}, u32[]{:S(2)}) %all-to-all-start.2) | async-done | bytes 524320 | tf_op jit(solution)/shard_map/all_to_all | solution.py:74
  267.4 33.5 %all-gather.4.cloned.1.call-done = bf16[2,8,128,1,16,128]{5,2,3,1,0,4:T(8,128)(2,1)} async-done(((bf16[2,8,128,1,1,128]{5,2,3,1,0,4:T(8,128)(2,1)}), bf16[2,8,128,1,16,128]{5,2,3,1,0,4:T(8,128)(2,1)}) %all-gather.4.cloned.1.call-update) | async-done | bytes 8388624 | tf_op jit(solution)/shard_map/all_gather | solution.py:68
  300.9 13.1 copy.42
  314.0 18.0 %reshape.518 = f32[2048,2048]{0,1:T(8,128)} reshape(f32[2,8,128,1,16,128]{2,1,0,5,4,3:T(8,128)} %copy.42) | data formatting | bytes 33554432 | tf_op jit(solution)/shard_map/convert_element_type | solution.py:69
  332.0 17.6 %copy.43 = f32[2048,2048]{1,0:T(8,128)} copy(f32[2048,2048]{0,1:T(8,128)} %reshape.518) | data formatting | bytes 33554432 | tf_op jit(solution)/shard_map/convert_element_type | solution.py:69
  349.6 11.9 fusion
  367.2 11.7 cholesky.457
  401.9 12.1 cholesky.480
  431.1 11.7 cholesky.503
  460.3 11.7 cholesky.524
  489.9 11.7 cholesky.962
  519.8 12.1 cholesky.982
  550.3 11.7 cholesky.1002
  580.8 11.7 cholesky.1022
  611.2 11.7 cholesky.1042
  641.7 11.7 cholesky.1062
  671.7 11.7 cholesky.1082
  700.9 11.9 cholesky.1102
  729.8 11.7 cholesky.1122
  785.6 11.9 cholesky.1162
  835.4 16.0 %fusion.1 = (f32[2048,2048]{1,0:T(8,128)}, bf16[2048,2048]{1,0:T(8,128)(2,1)}) fusion(f32[2048,2048]{1,0:T(8,128)} %get-tuple-element.135, pred[]{:T(512)S(6)} %cholesky.1203), kind=kLoop, calls=%fused_computation.9 | loop fusion | flops 20971520 | bytes 41943040 | tf_op jit(solution)/shard_map/triangular_solve | solution.py:75
  851.5 56.5 %while.1 = (s32[]{:T(128)}, f32[2048,2048]{1,0:T(8,128)}, s32[16,2]{0,1:T(2,128)S(1)}, f32[16,128,128]{2,1,0:T(8,128)}, s32[]{:T(128)}) while((s32[]{:T(128)}, f32[2048,2048]{1,0:T(8,128)}, s32[16,2]{0,1:T(2,128)S(1)}, f32[16,128,128]{2,1,0:T(8,128)}, s32[]{:T(128)}) %tuple.163), condition=%wide.while_cond, body=%wide.while_body.sunk | while | flops 2 | bytes 132705 | solution.py:75
  908.0 158.8 %custom-call.141 = f32[16,128,128]{1,2,0:T(8,128)} custom-call(f32[16,128,128]{2,1,0:T(8,128)} %get-tuple-element.12), custom_call_target="InvertDiagBlocksLowerTriangular" | custom-call | tf_op jit(solution)/shard_map/triangular_solve | solution.py:75
  1124.3 52.8 %all-gather.6.cloned.1.call-done = bf16[16,128,2048]{2,1,0:T(8,128)(2,1)} async-done(((bf16[1,128,2048]{2,1,0:T(8,128)(2,1)}), bf16[16,128,2048]{2,1,0:T(8,128)(2,1)}) %all-gather.6.cloned.1.call-update) | async-done | bytes 8388624 | tf_op jit(solution)/shard_map/all_gather | solution.py:89
  1181.6 12.4 copy.49
  1195.5 171.6 %all-reduce.4.cloned.1.call-done = bf16[8,128,2048]{2,1,0:T(8,128)(2,1)} async-done(((bf16[8,128,2048]{2,1,0:T(8,128)(2,1)}), bf16[8,128,2048]{2,1,0:T(8,128)(2,1)}) %all-reduce.4.cloned.1.call-update) | async-done | bytes 4194320 | tf_op jit(solution)/shard_map/psum | solution.py:12
  (241 shorter events, 487.5 us)
Async XLA Ops:
  11.0 36.3 %all-to-all-start = ((s32[128,1,2]{2,1,0:T(1,128)}), s32[128,1,2]{2,1,0:T(1,128)S(1)}, u32[]{:S(2)}, u32[]{:S(2)}) async-start(s32[128,1,2]{2,1,0:T(1,128)} %bitcast.7), calls=%async_computation | async-start | bytes 131072 | tf_op jit(solution)/shard_map/all_to_all | solution.py:46
  47.3 108.9 %all-to-all-start.1 = ((bf16[128,2,128,128]{3,2,1,0:T(8,128)(2,1)}), bf16[128,2,128,128]{3,2,1,0:T(8,128)(2,1)}, u32[]{:S(2)}, u32[]{:S(2)}) async-start(bf16[128,2,128,128]{3,2,1,0:T(8,128)(2,1)} %bitcast.328), calls=%async_computation.1 | async-start | bytes 16777216 | tf_op jit(solution)/shard_map/all_to_all | solution.py:39
  57.6 243.4 %all-gather.4.cloned.1.call-start = ((), (), s32[]{:S(2)}) async-start(), calls=%async_computation.3 | async-start | bytes 8912896 | tf_op jit(solution)/shard_map/all_gather | solution.py:68
  198.9 2.0 copy-start.1
  238.7 28.1 %all-to-all-start.2 = ((bf16[16,128,1,1,128]{4,1,3,2,0:T(8,128)(2,1)}), bf16[16,128,1,1,128]{4,1,3,2,0:T(8,128)(2,1)S(1)}, u32[]{:S(2)}, u32[]{:S(2)}) async-start(bf16[16,128,1,1,128]{4,1,3,2,0:T(8,128)(2,1)} %bitcast.321), calls=%async_computation.2 | async-start | bytes 1048576 | tf_op jit(solution)/shard_map/all_to_all | solution.py:74
  252.5 924.7 %all-gather.6.cloned.1.call-start = ((), (), s32[]{:S(2)}) async-start(), calls=%async_computation.4 | async-start | bytes 8912896 | tf_op jit(solution)/shard_map/all_gather | solution.py:89
  361.5 5.7 copy-start
  1124.2 242.9 %all-reduce.4.cloned.1.call-start = ((), (), s32[]{:S(2)}) async-start(), calls=%async_computation.5 | async-start | bytes 8388608 | tf_op jit(solution)/shard_map/psum | solution.py:12
  1367.1 11.3 copy-start.2
Sparse Core Ops, SparseCore 0:
  234.8 66.0 all-gather.3
  1124.4 52.7 all-gather.5
  1181.7 185.3 all-reduce.3
where the time goes:
time: 1400 us; the launch traced here: 1390 us
  other arithmetic  562 us (40%)
  waiting for transfers between devices  369 us (26%)
  local copies, waits for them, and re-layouts  210 us (15%)
  matrix products  160 us (11%)
  starting transfers between devices  36.1 us (3%)
  blocking collectives  32.8 us (2%)
  between operations  24.5 us (2%)
    another operation x63, other arithmetic, per_device(): jnp.linalg.cholesky(corner.reshape(PANEL, PANEL).astype(jnp.float32))  357 us
    another operation x3, other arithmetic, per_device(): lax.linalg.triangular_solve(lower_factor, mine.reshape(share_tiles * tile...  175 us
    psum x1, waiting for transfers between devices, spread(): return lax.psum(block, axis)  172 us
    all_to_all x1, waiting for transfers between devices, per_device(): lax.all_to_all(packed.reshape(device_count, CAP, tile_size, tile_size), (...  96.8 us
    another operation x30, matrix products, per_device(): jnp.linalg.cholesky(corner.reshape(PANEL, PANEL).astype(jnp.float32))  92.4 us
    another operation x48, local copies, waits for them, and re-layouts  56.5 us
    all_gather x1, waiting for transfers between devices, per_device(): lax.all_gather(solved_part.reshape(share_tiles, tile_size, PANEL), 'col',...  52.8 us
    another operation x31, matrix products, per_device(): lax.linalg.triangular_solve(lower_factor, mine.reshape(share_tiles * tile...  49.3 us
  transfers between devices with their start and end apart: 6, of which 5 were waited for; matrix products, arithmetic and copies ran while one was open for 3% of the time, Pallas kernels for 0%

commit v1 on v0

v1 whole, which is shorter than its diff:
```python
import jax
import jax.numpy as jnp
from jax import lax
from jax.experimental import pallas as pl
from jax.experimental.pallas import tpu as pltpu

from jax.sharding import PartitionSpec as P

CAP = 2
PANEL = 2048
TILE = 128
NT_DIMS = (((1,), (1,)), ((), ()))


def split2(x):
    hi = x.astype(jnp.bfloat16)
    lo = (x - hi.astype(jnp.float32)).astype(jnp.bfloat16)
    return hi, lo


def nt(a, b):
    return lax.dot_general(a, b, NT_DIMS, preferred_element_type=jnp.float32)


def invert_tile(a_ref, i_ref, out_ref):
    row = lax.broadcasted_iota(jnp.int32, (TILE, TILE), 0)
    col = lax.broadcasted_iota(jnp.int32, (TILE, TILE), 1)
    i_ref[...] = (row == col).astype(jnp.float32)
    full = (8, TILE)
    for g in range(TILE // 8):
        base = 8 * g
        group = a_ref[base : base + 8, :]
        cols = [jnp.broadcast_to(group[:, base + k : base + k + 1], full) for k in range(8)]
        d = {}
        for k in range(8):
            for i in range(k, 8):
                d[i, k] = jnp.broadcast_to(cols[k][i : i + 1, :], full)
        rs = {}
        lo = {}
        t = {}
        for j in range(8):
            rs[j] = lax.rsqrt(d[j, j])
            for i in range(j + 1, 8):
                lo[i, j] = d[i, j] * rs[j]
            for k in range(j + 1, 8):
                for i in range(k, 8):
                    d[i, k] = d[i, k] - lo[i, j] * lo[k, j]
            t[j, j] = rs[j]
            for m in range(j):
                acc = lo[j, m] * t[m, m]
                for k in range(m + 1, j):
                    acc = acc + lo[j, k] * t[k, m]
                t[j, m] = -(acc * rs[j])
        ga = [jnp.broadcast_to(a_ref[base + j : base + j + 1, :], full) for j in range(8)]
        gi = [jnp.broadcast_to(i_ref[base + j : base + j + 1, :], full) for j in range(8)]

        def lower(rows):
            out = []
            for i in range(8):
                acc = t[i, 0] * rows[0]
                for j in range(1, i + 1):
                    acc = acc + t[i, j] * rows[j]
                out.append(acc)
            return out

        def upper(rows):
            out = []
            for j in range(8):
                acc = t[7, j] * rows[7]
                for i in range(6, j - 1, -1):
                    acc = acc + t[i, j] * rows[i]
                out.append(acc)
            return out

        ui = lower(gi)
        for i in range(8):
            out_ref[base + i : base + i + 1, :] = ui[i][0:1, :]
        if g == TILE // 8 - 1:
            break
        va = upper(lower(ga))
        vi = upper(ui)
        for h in range(g + 1, TILE // 8):
            rows = slice(8 * h, 8 * h + 8)
            block = a_ref[rows, :]
            acc_a = block
            acc_i = i_ref[rows, :]
            for j in range(8):
                c = jnp.broadcast_to(block[:, base + j : base + j + 1], full)
                acc_a = acc_a - c * va[j]
                acc_i = acc_i - c * vi[j]
            a_ref[rows, :] = acc_a
            i_ref[rows, :] = acc_i


def factor_kernel(place_ref, tiles_ref, own_ref, xh_ref, xl_ref, m_ref, e_ref, f1_ref, f2_ref, a_ref, i_ref, t_ref):
    nt_ = PANEL // TILE
    half = nt_ // 2
    m_ref[...] = jnp.zeros_like(m_ref)
    for j in range(nt_):
        for i in range(j, nt_):
            m_ref[j // 2, i * TILE : (i + 1) * TILE, (j % 2) * TILE : (j % 2 + 1) * TILE] = tiles_ref[
                (i % 8) * 16 + j, i // 8
            ].astype(jnp.float32)
    own_ref[...] = jnp.zeros_like(own_ref)
    r = place_ref[0]
    c = place_ref[1]

    def step(k, carry):
        pair = k // 2
        lane = pl.multiple_of((k % 2) * TILE, TILE)
        top = pl.multiple_of(k * TILE, TILE)
        a_ref[...] = m_ref[pair, pl.ds(top, TILE), pl.ds(lane, TILE)]
        invert_tile(a_ref, i_ref, t_ref)
        row = lax.broadcasted_iota(jnp.int32, (TILE, TILE), 0)
        col = lax.broadcasted_iota(jnp.int32, (TILE, TILE), 1)
        th, tl = split2(t_ref[...])
        tt1 = jnp.concatenate([th, th], 1)
        tt2 = jnp.concatenate([tl, tl], 1)
        orig = m_ref[pair, pl.ds(top, TILE), pl.ds(lane, TILE)]
        oh, ol = split2(orig)
        oo = jnp.concatenate([oh, ol], 1)
        diag = nt(oo, tt1) + nt(oo, tt2)
        diag = jnp.where(row >= col, diag, 0.0).astype(jnp.bfloat16)
        m_ref[pair, pl.ds(top, TILE), pl.ds(lane, TILE)] = (row == col).astype(jnp.float32)

        for q in range(half):
            @pl.when(2 * q + 1 > k)
            def _():
                lane_tile = lax.broadcasted_iota(jnp.int32, (TILE, 2 * TILE), 1) // TILE + 2 * q
                m_ref[q, pl.ds(top, TILE), :] = jnp.where(
                    lane_tile > k, 0.0, m_ref[q, pl.ds(top, TILE), :]
                )

        def column(b, carry):
            rows = pl.ds(pl.multiple_of(b * 256, 256), 256)
            ch, cl = split2(m_ref[pair, rows, pl.ds(lane, TILE)])
            cc = jnp.concatenate([ch, cl], 1)
            e = nt(cc, tt1) + nt(cc, tt2)
            eh, el = split2(e)
            e_ref[rows, 0:TILE] = eh
            e_ref[rows, TILE:] = el
            tile = b * 2 + lax.broadcasted_iota(jnp.int32, (256, TILE), 0) // TILE
            zero = jnp.zeros((256, TILE), jnp.bfloat16)
            fh = jnp.where(tile > k, eh, zero)
            fl = jnp.where(tile > k, el, zero)
            f1_ref[rows, 0:TILE] = fh
            f1_ref[rows, TILE:] = fh
            f2_ref[rows, 0:TILE] = fl
            f2_ref[rows, TILE:] = fl
            xh_ref[rows, pl.ds(top, TILE)] = jnp.where(tile > k, zero, eh)
            xl_ref[rows, pl.ds(top, TILE)] = jnp.where(tile > k, zero, el)
            return carry

        lax.fori_loop(0, half, column, 0, unroll=True)

        @pl.when(k == c)
        def _():
            for a in range(2):
                i = r + a * 8
                src = e_ref[pl.ds(pl.multiple_of(i * TILE, TILE), TILE), 0:TILE]
                own_ref[a] = jnp.where(i == k, diag, jnp.where(i > k, src, jnp.zeros_like(src)))

        def update(q, carry):
            cols = pl.ds(pl.multiple_of(q * 256, 256), 256)
            f1 = f1_ref[cols, :]
            f2 = f2_ref[cols, :]
            for b in range(PANEL // 512):
                rows = pl.ds(b * 512, 512)
                ee = e_ref[rows, :]
                m_ref[q, rows, :] = m_ref[q, rows, :] - (nt(ee, f1) + nt(ee, f2))
            return carry

        lax.fori_loop((k + 1) // 2, half, update, 0)
        return carry

    lax.fori_loop(0, nt_, step, 0)


def factor_corner(tiles, place):
    vm = pl.BlockSpec(memory_space=pltpu.VMEM)
    return pl.pallas_call(
        factor_kernel,
        out_shape=(
            jax.ShapeDtypeStruct((2, TILE, TILE), jnp.bfloat16),
            jax.ShapeDtypeStruct((PANEL, PANEL), jnp.bfloat16),
            jax.ShapeDtypeStruct((PANEL, PANEL), jnp.bfloat16),
        ),
        in_specs=[pl.BlockSpec(memory_space=pltpu.SMEM), vm],
        out_specs=(vm, vm, vm),
        scratch_shapes=[
            pltpu.VMEM((8, PANEL, 256), jnp.float32),
            pltpu.VMEM((PANEL, 256), jnp.bfloat16),
            pltpu.VMEM((PANEL, 256), jnp.bfloat16),
            pltpu.VMEM((PANEL, 256), jnp.bfloat16),
            pltpu.VMEM((TILE, TILE), jnp.float32),
            pltpu.VMEM((TILE, TILE), jnp.float32),
            pltpu.VMEM((TILE, TILE), jnp.float32),
        ],
        compiler_params=pltpu.CompilerParams(vmem_limit_bytes=60 * 1024 * 1024),
        cost_estimate=pl.CostEstimate(flops=100_000_000_000, bytes_accessed=24_000_000, transcendentals=0),
        name="factor_corner",
    )(place, tiles)


def pack_kernel(slot_ref, child_ref, packed_ref, sem):
    count = child_ref.shape[0]

    def start(t, carry):
        pltpu.make_async_copy(child_ref.at[t], packed_ref.at[slot_ref[t]], sem).start()
        return carry

    lax.fori_loop(0, count, start, 0)
    pltpu.make_async_copy(child_ref, packed_ref.at[pl.ds(0, count)], sem).wait()


def pack(slots, child_tiles):
    count = child_tiles.shape[0]
    return pl.pallas_call(
        pack_kernel,
        out_shape=jax.ShapeDtypeStruct((CAP * count, TILE, TILE), jnp.bfloat16),
        in_specs=[pl.BlockSpec(memory_space=pltpu.SMEM), pl.BlockSpec(memory_space=pl.ANY)],
        out_specs=pl.BlockSpec(memory_space=pl.ANY),
        scratch_shapes=[pltpu.SemaphoreType.DMA],
        cost_estimate=pl.CostEstimate(flops=0, bytes_accessed=16_000_000, transcendentals=0),
        name="pack_tiles",
    )(slots, child_tiles)


def extend_kernel(id_ref, front_ref, arrived_ref, out_ref, panel_ref, acc_ref):
    cols_local = front_ref.shape[1] // TILE
    acc_ref[...] = front_ref[...].astype(jnp.float32)

    def add(s, carry):
        local = id_ref[s]

        @pl.when(local >= 0)
        def _():
            rows = pl.ds(pl.multiple_of(local // cols_local * TILE, TILE), TILE)
            cols = pl.ds(pl.multiple_of(local % cols_local * TILE, TILE), TILE)
            acc_ref[rows, cols] = acc_ref[rows, cols] + arrived_ref[s].astype(jnp.float32)

        return carry

    lax.fori_loop(0, arrived_ref.shape[0], add, 0)
    total = acc_ref[...].astype(jnp.bfloat16)
    out_ref[...] = total
    panel_ref[...] = total[2 * TILE :, 0:TILE]


def extend(ids, front, arrived):
    vm = pl.BlockSpec(memory_space=pltpu.VMEM)
    return pl.pallas_call(
        extend_kernel,
        out_shape=(
            jax.ShapeDtypeStruct(front.shape, jnp.bfloat16),
            jax.ShapeDtypeStruct((front.shape[0] - 2 * TILE, TILE), jnp.bfloat16),
        ),
        in_specs=[pl.BlockSpec(memory_space=pltpu.SMEM), vm, vm],
        out_specs=(vm, vm),
        scratch_shapes=[pltpu.VMEM(front.shape, jnp.float32)],
        compiler_params=pltpu.CompilerParams(vmem_limit_bytes=48 * 1024 * 1024),
        cost_estimate=pl.CostEstimate(flops=10_000_000, bytes_accessed=30_000_000, transcendentals=0),
        name="extend_add",
    )(ids, front, arrived)


def finish_kernel(place_ref, xh_ref, xl_ref, row_ref, col_ref, own_ref, assembled_ref, out_ref, a_ref, p_ref):
    step = pl.program_id(0)
    rows_low = row_ref.shape[1] * TILE
    cols_low = col_ref.shape[1] * TILE
    total = rows_low + cols_low
    c = place_ref[1]
    width = 2 * TILE

    @pl.when(step == 0)
    def _():
        out_ref[...] = assembled_ref[...].astype(jnp.float32)
        out_ref[0 : 2 * TILE, :] = jnp.zeros((2 * TILE, out_ref.shape[1]), jnp.float32)
        for a in range(2):
            out_ref[a * TILE : (a + 1) * TILE, 0:TILE] = own_ref[a].astype(jnp.float32)

    for s in range(PANEL // width):

        @pl.when(step == s)
        def _():
            for piece in range(2):
                lanes = slice(s * width + piece * TILE, s * width + (piece + 1) * TILE)
                a_ref[0:rows_low, lanes] = row_ref[piece].reshape(rows_low, TILE)
                a_ref[rows_low:total, lanes] = col_ref[piece].reshape(cols_low, TILE)
            depth = (s + 1) * width
            chunk = total // 6

            def solve(b, carry):
                rows = pl.ds(pl.multiple_of(b * chunk, chunk), chunk)
                a = a_ref[rows, 0:depth]
                p = jnp.dot(a, xh_ref[0:depth, :], preferred_element_type=jnp.float32) + jnp.dot(
                    a, xl_ref[0:depth, :], preferred_element_type=jnp.float32
                )
                p_ref[rows, :] = p.astype(jnp.bfloat16)
                return carry

            lax.fori_loop(0, 6, solve, 0)

    @pl.when(step == c // 2)
    def _():
        lane = pl.multiple_of(c % 2 * TILE, TILE)
        out_ref[2 * TILE :, 0:TILE] = p_ref[0:rows_low, pl.ds(lane, TILE)].astype(jnp.float32)

    def update(b, carry):
        rows = pl.ds(pl.multiple_of(b * 256, 256), 256)
        u = lax.dot_general(
            p_ref[rows, :], p_ref[rows_low:total, :], NT_DIMS, preferred_element_type=jnp.float32
        )
        target = pl.ds(pl.multiple_of(b * 256 + 2 * TILE, 256), 256)
        out_ref[target, TILE:] = out_ref[target, TILE:] - u
        return carry

    lax.fori_loop(0, rows_low // 256, update, 0)


def finish(place, xh, xl, row_raw, col_raw, own, assembled):
    width = 2 * TILE
    tiles_row = row_raw.shape[1]
    tiles_col = col_raw.shape[1]
    total = (tiles_row + tiles_col) * TILE
    vm = pl.BlockSpec(memory_space=pltpu.VMEM)
    return pl.pallas_call(
        finish_kernel,
        grid=(PANEL // width,),
        out_shape=jax.ShapeDtypeStruct(assembled.shape, jnp.float32),
        in_specs=[
            pl.BlockSpec(memory_space=pltpu.SMEM),
            pl.BlockSpec((PANEL, width), lambda s: (0, s)),
            pl.BlockSpec((PANEL, width), lambda s: (0, s)),
            pl.BlockSpec((2, tiles_row, TILE, TILE), lambda s: (s, 0, 0, 0)),
            pl.BlockSpec((2, tiles_col, TILE, TILE), lambda s: (s, 0, 0, 0)),
            vm,
            vm,
        ],
        out_specs=vm,
        scratch_shapes=[
            pltpu.VMEM((total, PANEL), jnp.bfloat16),
            pltpu.VMEM((total, width), jnp.bfloat16),
        ],
        compiler_params=pltpu.CompilerParams(
            vmem_limit_bytes=56 * 1024 * 1024, dimension_semantics=("arbitrary",)
        ),
        cost_estimate=pl.CostEstimate(flops=40_000_000_000, bytes_accessed=50_000_000, transcendentals=0),
        name="solve_update",
    )(place, xh, xl, row_raw, col_raw, own, assembled)


def per_device(front, child_tiles, tile_map):
    rows_local = front.shape[0]
    cols_local = front.shape[3]
    row_count = lax.axis_size("row")
    col_count = lax.axis_size("col")
    device_count = row_count * col_count
    row_index = lax.axis_index("row")
    col_index = lax.axis_index("col")
    both = ("row", "col")
    corner = front[0:2, 0, :, 0, 0, :]
    corner = lax.all_gather(corner, both, axis=0, tiled=False)

    owners = tile_map[:, 0] % row_count * col_count + tile_map[:, 1] % col_count
    local_ids = tile_map[:, 0] // row_count * cols_local + tile_map[:, 1] // col_count
    owner_hits = (owners[:, None] == jnp.arange(device_count)[None, :]).astype(jnp.int32)
    slot_rank = jnp.sum(jnp.cumsum(owner_hits, 0) * owner_hits, 1) - 1
    slot_index = owners * CAP + slot_rank
    packed = pack(slot_index, child_tiles)
    targets = jnp.full((device_count * CAP,), -1, jnp.int32).at[slot_index].set(local_ids)
    arrived = lax.all_to_all(
        packed.reshape(device_count, CAP, TILE, TILE), both, split_axis=0, concat_axis=0, tiled=True
    )
    arrived_ids = lax.all_to_all(
        targets.reshape(device_count, CAP), both, split_axis=0, concat_axis=0, tiled=True
    )

    place = jnp.stack([row_index, col_index]).astype(jnp.int32)
    own, xh, xl = factor_corner(corner, place)

    assembled, panel = extend(
        arrived_ids.reshape(device_count * CAP),
        front.reshape(rows_local * TILE, cols_local * TILE),
        arrived.reshape(device_count * CAP, TILE, TILE),
    )
    low_tiles = rows_local - 2
    panel = panel.reshape(low_tiles, TILE, TILE)
    row_raw = lax.all_gather(panel, "col", axis=0, tiled=False)
    split_panel = panel.reshape(low_tiles // 2, 2, TILE, TILE)
    halves = (split_panel[:, 0], split_panel[:, 1])
    parity = col_index % 2
    received = []
    for k in range(2):
        pairs = []
        for r in range(row_count):
            for c in range(col_count):
                h = (c % 2) ^ k
                pairs.append((r * col_count + c, (c // 2) * col_count + row_count * h + r))
        outgoing = jnp.where(parity == k, halves[0], halves[1])
        received.append(lax.ppermute(outgoing, both, pairs))
    high = col_index // row_count
    first = jnp.where(high == 0, received[0], received[1])
    second = jnp.where(high == 0, received[1], received[0])
    col_raw = lax.all_gather(jnp.stack([first, second]), "row", axis=0, tiled=True)
    out = finish(place, xh, xl, row_raw, col_raw, own, assembled)
    return out.reshape(rows_local, 1, TILE, cols_local, 1, TILE)


def solution(mesh):
    in_specs = (
        P(None, "row", None, None, "col", None),
        P(("row", "col"), None, None),
        P(("row", "col"), None),
    )
    out_specs = P(None, "row", None, None, "col", None)
    return jax.shard_map(
        per_device, mesh=mesh, in_specs=in_specs, out_specs=out_specs, check_vma=False
    )
```

time: 1400 us -> 543 us (0.39)
  other arithmetic: 562 us -> 7.76 us
  Pallas kernels: 0 us -> 359 us
  waiting for transfers between devices: 369 us -> 116 us
  local copies, waits for them, and re-layouts: 210 us -> 20.3 us
  matrix products: 160 us -> 0 us
  blocking collectives: 32.8 us -> 0 us
    another operation x66 -> x3, other arithmetic: 532 us -> 1.46 us  [the longest x2 0.85 us: per_device(): jnp.stack([first, second])]
    pallas_call x0 -> x4, Pallas kernels: none -> 359 us  [the longest x1 155 us: factor_corner(): pl.pallas_call(factor_kernel, out_shape=(jax.ShapeDtypeStruct((2, TILE, T...]
    psum x1 -> x0, waiting for transfers between devices: 172 us -> none  [spread(): return lax.psum(block, axis)]
    another operation x61 -> x0, matrix products: 142 us -> none  [the longest x30 92.4 us: per_device(): jnp.linalg.cholesky(corner.reshape(PANEL, PANEL).astype(jnp.float32))]
    all_gather x2 -> x3, waiting for transfers between devices: 86.3 us -> 0.01 us  [the longest x1 0.01 us: per_device(): corner = lax.all_gather(corner, both, axis=0, tiled=False)]
    another operation x66 -> x0, local copies, waits for them, and re-layouts: 64.4 us -> none
    convert_element_type x4 -> x0, local copies, waits for them, and re-layouts: 49.7 us -> none  [the longest x3 48.7 us: per_device(): corner.reshape(PANEL, PANEL).astype(jnp.float32)]
    all_gather x1 -> x0, blocking collectives: 32.8 us -> none  [per_device(): corner = lax.all_gather(corner, 'row', axis=1, tiled=True)]
  transfers between devices with their start and end apart: 6 -> 7, of which waited for: 5 -> 3; matrix products, arithmetic and copies ran while one was open for 3% -> 3% of each run, Pallas kernels for 0% -> 55%
where the time goes in v1:
time: 543 us; the launch traced here: 540 us
  Pallas kernels  359 us (66%)
  waiting for transfers between devices  116 us (21%)
  starting transfers between devices  23.8 us (4%)
  local copies, waits for them, and re-layouts  20.3 us (4%)
  between operations  13.2 us (2%)
  other arithmetic  7.76 us (1%)
    pallas_call x1, Pallas kernels, factor_corner(): pl.pallas_call(factor_kernel, out_shape=(jax.ShapeDtypeStruct((2, TILE, T...  155 us
    pallas_call x1, Pallas kernels, pack(): pl.pallas_call(pack_kernel, out_shape=jax.ShapeDtypeStruct((CAP * count,...  129 us
    all_to_all x1, waiting for transfers between devices, per_device(): lax.all_to_all(packed.reshape(device_count, CAP, TILE, TILE), both, split...  91.8 us
    pallas_call x1, Pallas kernels, finish(): pl.pallas_call(finish_kernel, grid=(PANEL // width,), out_shape=jax.Shape...  63.5 us
    ppermute x2, waiting for transfers between devices, per_device(): received.append(lax.ppermute(outgoing, both, pairs))  23.3 us
    unnamed x5, local copies, waits for them, and re-layouts  16.8 us
    pallas_call x1, Pallas kernels, extend(): pl.pallas_call(extend_kernel, out_shape=(jax.ShapeDtypeStruct(front.shape...  12.4 us
    all_to_all x1, starting transfers between devices, per_device(): lax.all_to_all(targets.reshape(device_count, CAP), both, split_axis=0, co...  11.5 us
  transfers between devices with their start and end apart: 7, of which 3 were waited for; matrix products, arithmetic and copies ran while one was open for 3% of the time, Pallas kernels for 55%

profile of v1, /device:TPU:1, one launch (start us, length us, event | category | flops | bytes accessed | tf_op | source)
XLA Modules:
  0.0 540.3 jit_solution(3975089862880710888)
XLA Ops:
  6.5 1.1 slice.17
  7.7 0.6 copy.15
  8.3 0.8 fusion.11
  9.1 0.1 fusion.1
  9.2 0.2 reduce_window_sum.11
  9.3 0.2 select_reduce_fusion
  9.5 0.8 fusion.8
  10.3 1.3 multiply_add_fusion
  11.6 1.0 scatter_custom_fusion
  12.6 0.8 all_to_all.9
  13.4 11.5 %all-to-all-start = ((s32[128,1,2]{2,1,0:T(1,128)}), s32[128,1,2]{2,1,0:T(1,128)S(1)}, u32[]{:S(2)}, u32[]{:S(2)}) async-start(s32[128,1,2]{2,1,0:T(1,128)} %bitcast.8), calls=%async_computation | async-start | bytes 131072 | tf_op jit(solution)/shard_map/all_to_all | solution.py:375
  24.9 128.8 %pack_tiles.1 = bf16[256,128,128]{2,1,0:T(8,128)(2,1)} custom-call(s32[128]{0:T(128)} %get-tuple-element.17.slot_ref, bf16[128,128,128]{2,1,0:T(8,128)(2,1)} %child_ref.1), custom_call_target="tpu_custom_call" | custom-call | bytes 16000000 | tf_op jit(solution)/shard_map/pack_tiles/pallas_call | solution.py:218
  153.7 10.2 %all-to-all-start.1 = ((bf16[128,2,128,128]{3,2,1,0:T(8,128)(2,1)}), bf16[128,2,128,128]{3,2,1,0:T(8,128)(2,1)}, u32[]{:S(2)}, u32[]{:S(2)}) async-start(bf16[128,2,128,128]{3,2,1,0:T(8,128)(2,1)} %bitcast.78), calls=%async_computation.1 | async-start | bytes 16777216 | tf_op jit(solution)/shard_map/all_to_all | solution.py:372
  164.0 5.2 copy.20
  169.2 0.6 broadcast.102
  169.8 0.8 reduce.3
  170.7 0.1 reshape.33.id_ref
  170.8 91.8 %all-to-all-done.1 = bf16[128,2,128,128]{3,2,1,0:T(8,128)(2,1)} async-done(((bf16[128,2,128,128]{3,2,1,0:T(8,128)(2,1)}), bf16[128,2,128,128]{3,2,1,0:T(8,128)(2,1)}, u32[]{:S(2)}, u32[]{:S(2)}) %all-to-all-start.1) | async-done | bytes 8388640 | tf_op jit(solution)/shard_map/all_to_all | solution.py:372
  262.6 12.4 %extend_add.1 = (bf16[2048,1024]{1,0:T(8,128)(2,1)S(1)}, bf16[1792,128]{1,0:T(8,128)(2,1)}) custom-call(s32[256]{0:T(256)S(1)} %reshape.33.id_ref, bf16[2048,1024]{1,0:T(8,128)(2,1)} %bitcast.79, bf16[256,128,128]{2,1,0:T(8,128)(2,1)} %bitcast.10.arrived_ref), custom_call_target="tpu_custom_call" | custom-call | flops 10000000 | bytes 30000000 | tf_op jit(solution)/shard_map/extend_add/pallas_call | solution.py:252
  275.0 2.1 copy-done
  277.1 1.1 fusion
  278.2 1.9 collective-permute-start
  280.1 1.1 select_bitcast_fusion.2
  281.2 0.1 collective-permute-start.1
  281.3 22.4 %collective-permute-done = bf16[7,128,128]{2,1,0:T(8,128)(2,1)S(1)} collective-permute-done((bf16[7,128,128]{2,1,0:T(8,128)(2,1)S(1)}, bf16[7,128,128]{2,1,0:T(8,128)(2,1)S(1)}, u32[]{:S(2)}, u32[]{:S(2)}) %collective-permute-start) | collective-permute-done | bytes 229408 | tf_op jit(solution)/shard_map/ppermute | solution.py:401
  303.7 0.9 collective-permute-done.1
  304.7 0.8 pad_maximum_fusion
  305.6 0.7 all-gather.5.cloned.1.call-update
  306.2 0.6 pad_add_fusion.place_ref
  306.9 154.6 %factor_corner.1 = (bf16[2,128,128]{2,1,0:T(8,128)(2,1)}, bf16[2048,2048]{1,0:T(8,128)(2,1)}, bf16[2048,2048]{1,0:T(8,128)(2,1)}) custom-call(s32[2]{0:T(128)} %pad_add_fusion.place_ref, bf16[128,2,128,128]{3,2,1,0:T(8,128)(2,1)} %bitcast.82), custom_call_target="tpu_custom_call" | custom-call | flops 99999997952 | bytes 24000000 | tf_op jit(solution)/shard_map/factor_corner/pallas_call | solution.py:181
  461.4 63.5 %solve_update.1 = f32[2048,1024]{1,0:T(8,128)} custom-call(s32[2]{0:T(128)} %pad_add_fusion.place_ref, bf16[2048,2048]{1,0:T(8,128)(2,1)} %get-tuple-element.10.xh_ref, bf16[2048,2048]{1,0:T(8,128)(2,1)} %get-tuple-element.11.xl_ref, bf16[16,14,128,128]{3,2,1,0:T(8,128)(2,1)} %all-gather.5.cloned.1.call-done.row_ref, ...), custom_call_target="tpu_custom_call" | custom-call | flops 40000000000 | bytes 50000000 | tf_op jit(solution)/shard_map/solve_update/pallas_call | solution.py:327
  524.9 8.9 %copy.18 = f32[256,8,8,128]{3,2,1,0:T(8,128)} copy(f32[256,8,8,128]{3,1,2,0:T(8,128)} %bitcast.80) | data formatting | bytes 16777216
  (11 shorter events, 0.2 us)
Async XLA Ops:
  6.5 300.3 %all-gather.9.cloned.1.call-start = ((), (), s32[]{:S(2)}) async-start(), calls=%async_computation.4 | async-start | bytes 8454144 | tf_op jit(solution)/shard_map/all_gather | solution.py:363
  13.4 140.3 %all-to-all-start = ((s32[128,1,2]{2,1,0:T(1,128)}), s32[128,1,2]{2,1,0:T(1,128)S(1)}, u32[]{:S(2)}, u32[]{:S(2)}) async-start(s32[128,1,2]{2,1,0:T(1,128)} %bitcast.8), calls=%async_computation | async-start | bytes 131072 | tf_op jit(solution)/shard_map/all_to_all | solution.py:375
  153.7 108.9 %all-to-all-start.1 = ((bf16[128,2,128,128]{3,2,1,0:T(8,128)(2,1)}), bf16[128,2,128,128]{3,2,1,0:T(8,128)(2,1)}, u32[]{:S(2)}, u32[]{:S(2)}) async-start(bf16[128,2,128,128]{3,2,1,0:T(8,128)(2,1)} %bitcast.78), calls=%async_computation.1 | async-start | bytes 16777216 | tf_op jit(solution)/shard_map/all_to_all | solution.py:372
  164.0 297.5 %all-gather.7.cloned.1.call-start = ((), (), s32[]{:S(2)}) async-start(), calls=%async_computation.3 | async-start | bytes 4128768 | tf_op jit(solution)/shard_map/all_gather | solution.py:405
  275.0 2.1 copy-start
  278.2 25.6 %collective-permute-start = (bf16[7,128,128]{2,1,0:T(8,128)(2,1)S(1)}, bf16[7,128,128]{2,1,0:T(8,128)(2,1)S(1)}, u32[]{:S(2)}, u32[]{:S(2)}) collective-permute-start(bf16[7,128,128]{2,1,0:T(8,128)(2,1)S(1)} %fusion), channel_id=1, source_target_pairs={{0,0},{1,8},{2,16},{3,24},{4,32},{5,40},{6,48},{7,56},{8,64},{9,72... | collective-permute-start | bytes 688136 | tf_op jit(solution)/shard_map/ppermute | solution.py:401
  281.2 23.5 %collective-permute-start.1 = (bf16[7,128,128]{2,1,0:T(8,128)(2,1)S(1)}, bf16[7,128,128]{2,1,0:T(8,128)(2,1)S(1)}, u32[]{:S(2)}, u32[]{:S(2)}) collective-permute-start(bf16[7,128,128]{2,1,0:T(8,128)(2,1)S(1)} %select_bitcast_fusion.2), channel_id=1, source_target_pairs={{0,8},{1,0},{2,24},{3,16},{4,40},{5,32},{6,56},{7,48},{8,72},{9,64... | collective-permute-start | bytes 688136 | tf_op jit(solution)/shard_map/ppermute | solution.py:401
  305.5 155.9 %all-gather.5.cloned.1.call-start = ((), (), s32[]{:S(2)}) async-start(), calls=%async_computation.2 | async-start | bytes 7798784 | tf_op jit(solution)/shard_map/all_gather | solution.py:389
Sparse Core Ops, SparseCore 0:
  10.3 73.7 all-gather.8
  305.6 72.0 all-gather.6
  379.5 45.6 all-gather.4

commit v2 on v1

v2 whole, which is shorter than its diff:
```python
import functools
import numpy as np
import jax
import jax.numpy as jnp
from jax import lax
from jax.experimental import pallas as pl
from jax.experimental.pallas import tpu as pltpu
from jax.sharding import PartitionSpec as P

CAP = 2
PANEL = 2048
TILE = 128
NT_DIMS = (((1,), (1,)), ((), ()))


def split2(x):
    hi = x.astype(jnp.bfloat16)
    lo = (x - hi.astype(jnp.float32)).astype(jnp.bfloat16)
    return hi, lo


def nt(a, b):
    return lax.dot_general(a, b, NT_DIMS, preferred_element_type=jnp.float32)


def spread8(x):
    return jnp.broadcast_to(x, (8, TILE))


def total(terms):
    acc = terms[0]
    for term in terms[1:]:
        acc = acc + term
    return acc


def invert_tile(a_ref, i_ref, s_ref, out_ref, beside):
    row = lax.broadcasted_iota(jnp.int32, (TILE, TILE), 0)
    col = lax.broadcasted_iota(jnp.int32, (TILE, TILE), 1)
    i_ref[...] = (row == col).astype(jnp.float32)
    steps = TILE // 8
    for g in range(steps):
        base = 8 * g
        group = a_ref[base : base + 8, :]
        for k in range(8):
            s_ref[8 * k : 8 * k + 8, :] = spread8(group[:, base + k : base + k + 1])
        d = {}
        for k in range(8):
            for i in range(k, 8):
                d[i, k] = spread8(s_ref[8 * k + i : 8 * k + i + 1, :])
        ga = [spread8(a_ref[base + j : base + j + 1, :]) for j in range(8)]
        gi = [spread8(i_ref[base + j : base + j + 1, :]) for j in range(8)]
        rs = {}
        lo = {}
        for j in range(0, 8, 2):
            rs[j] = lax.rsqrt(d[j, j])
            det = lax.rsqrt(d[j, j] * d[j + 1, j + 1] - d[j + 1, j] * d[j + 1, j])
            rs[j + 1] = det * (d[j, j] * rs[j])
            lo[j + 1, j] = d[j + 1, j] * rs[j]
            for i in range(j + 2, 8):
                lo[i, j] = d[i, j] * rs[j]
                lo[i, j + 1] = (d[i, j + 1] - lo[i, j] * lo[j + 1, j]) * rs[j + 1]
            for k in range(j + 2, 8):
                for i in range(k, 8):
                    d[i, k] = d[i, k] - (lo[i, j] * lo[k, j] + lo[i, j + 1] * lo[k, j + 1])
        t = {}
        for j in range(8):
            t[j, j] = rs[j]
            for m in range(j):
                t[j, m] = -(total([lo[j, k] * t[k, m] for k in range(m, j)]) * rs[j])
        ui = [total([t[i, j] * gi[j] for j in range(i + 1)]) for i in range(8)]
        for i in range(8):
            out_ref[base + i : base + i + 1, :] = ui[i][0:1, :]
        if g < steps - 1:
            ua = [total([t[i, j] * ga[j] for j in range(i + 1)]) for i in range(8)]
            va = [total([t[i, j] * ua[i] for i in range(j, 8)]) for j in range(8)]
            vi = [total([t[i, j] * ui[i] for i in range(j, 8)]) for j in range(8)]
        for h in range(g + 1, steps):
            rows = slice(8 * h, 8 * h + 8)
            block = a_ref[rows, :]
            acc_a = block
            acc_i = i_ref[rows, :]
            for j in range(8):
                c = spread8(block[:, base + j : base + j + 1])
                acc_a = acc_a - c * va[j]
                acc_i = acc_i - c * vi[j]
            a_ref[rows, :] = acc_a
            i_ref[rows, :] = acc_i
        beside(g)


def unit_table(first, last):
    pairs = PANEL // 256
    count = pairs - first
    table = np.full((pairs + 1, 64), count * 8, np.int32)
    lengths = np.zeros((pairs + 1,), np.int32)
    for p in range(first, last + 1):
        units = []
        prev = p - 1
        start = p + 1 if p < last else p
        if prev >= first:
            for q in range(start, pairs):
                units += [(q - first) * 8 + b for b in range(pairs) if b <= prev or b >= q]
        lengths[p] = len(units)
        table[p, : len(units)] = units
    return np.concatenate([table.reshape(-1), lengths])


SLOTS = 64


def factor_kernel(first, last, place_ref, unit_ref, source_ref, own_ref, xh_ref, xl_ref, *rest):
    tiles = PANEL // TILE
    pairs = tiles // 2
    if last < pairs:
        next_ref, rest = rest[0], rest[1:]
    m_ref, eh_ref, el_ref, a_ref, o_ref, i_ref, s_ref, t_ref, sem = rest
    if first == 0:
        for j in range(tiles):
            for i in range(tiles):
                spot = (j // 2, slice(i * TILE, (i + 1) * TILE), slice(j % 2 * TILE, (j % 2 + 1) * TILE))
                if i >= j:
                    m_ref[spot] = source_ref[i % 8 * 16 + j, i // 8].astype(jnp.float32)
                else:
                    m_ref[spot] = jnp.zeros((TILE, TILE), jnp.float32)
    else:
        load = pltpu.make_async_copy(source_ref, m_ref.at[pl.ds(0, pairs - first)], sem)
        load.start()
        load.wait()
    own_ref[...] = jnp.zeros_like(own_ref)
    r = place_ref[0]
    c = place_ref[1]
    row = lax.broadcasted_iota(jnp.int32, (TILE, TILE), 0)
    col = lax.broadcasted_iota(jnp.int32, (TILE, TILE), 1)
    identity = (row == col).astype(jnp.float32)
    zero = jnp.zeros((TILE, TILE), jnp.bfloat16)

    def product(rows, cols, buf):
        lh, ll = eh_ref[buf, rows, :], el_ref[buf, rows, :]
        rh, rl = eh_ref[buf, cols, :], el_ref[buf, cols, :]
        return nt(lh, rh) + nt(lh, rl) + nt(ll, rh)

    def block_rows(b):
        return pl.ds(pl.multiple_of(b * 256, 256), 256)

    def tile_rows(i):
        return pl.ds(pl.multiple_of(i * TILE, TILE), TILE)

    def apply(code, buf):
        q = code // 8
        rows = block_rows(code % 8)
        cols = block_rows(jnp.minimum(q + first, pairs - 1))
        m_ref[q, rows, :] = m_ref[q, rows, :] - product(rows, cols, buf)

    def keep_own(k, buf, half):
        th, tl = split2(t_ref[...])
        oh, ol = split2(o_ref[...])
        both = jnp.concatenate([oh, ol], 1)
        diag = nt(both, jnp.concatenate([th, th], 1)) + nt(both, jnp.concatenate([tl, tl], 1))
        diag = jnp.where(row >= col, diag, 0.0).astype(jnp.bfloat16)

        @pl.when(k == c)
        def _():
            for a in range(2):
                i = r + a * 8
                src = eh_ref[buf, tile_rows(i), half * TILE : (half + 1) * TILE]
                own_ref[a] = jnp.where(i == k, diag, jnp.where(i > k, src, zero))

    def column(p, buf, half):
        th, tl = split2(t_ref[...])
        tt1 = jnp.concatenate([th, th], 1)
        tt2 = jnp.concatenate([tl, tl], 1)
        lanes = slice(half * TILE, (half + 1) * TILE)
        for b in range(pairs):
            rows = slice(b * 256, (b + 1) * 256)
            ch, cl = split2(m_ref[p - first, rows, lanes])
            both = jnp.concatenate([ch, cl], 1)
            eh, el = split2(nt(both, tt1) + nt(both, tt2))
            eh_ref[buf, rows, lanes] = eh
            el_ref[buf, rows, lanes] = el

    def step(p, carry):
        local = p - first
        buf = p % 2
        old = 1 - buf
        k = 2 * p
        m_ref[local, tile_rows(k), TILE:] = jnp.zeros((TILE, TILE), jnp.float32)

        diag = m_ref[local, tile_rows(k), 0:TILE]
        if first == 0:
            new = diag - product(tile_rows(k), tile_rows(k), old)
            diag = jnp.where(p > first, new, diag)
        else:
            new = diag - product(tile_rows(k), tile_rows(k), old)
            diag = jnp.where(p > first, new, diag)
        a_ref[...] = diag
        o_ref[...] = diag

        def first_beside(g):
            if g < 8:
                rows = slice(g * 256, (g + 1) * 256)
                old_block = m_ref[local, rows, :]
                new_block = old_block - product(rows, block_rows(p), old)
                m_ref[local, rows, :] = jnp.where(p > first, new_block, old_block)
            else:
                apply(unit_ref[p * SLOTS + g - 8], old)

        invert_tile(a_ref, i_ref, s_ref, t_ref, first_beside)
        m_ref[local, tile_rows(k), 0:TILE] = identity
        m_ref[local, tile_rows(k), TILE:] = jnp.zeros((TILE, TILE), jnp.float32)
        column(p, buf, 0)
        keep_own(k, buf, 0)

        def pair_product(rows):
            h = eh_ref[buf, rows, 0:TILE]
            l = el_ref[buf, rows, 0:TILE]
            fh = eh_ref[buf, tile_rows(k + 1), 0:TILE]
            fl = el_ref[buf, tile_rows(k + 1), 0:TILE]
            both = jnp.concatenate([h, l], 1)
            return nt(both, jnp.concatenate([fh, fh], 1)) + nt(both, jnp.concatenate([fl, fl], 1))

        diag = m_ref[local, tile_rows(k + 1), TILE:] - pair_product(tile_rows(k + 1))
        a_ref[...] = diag
        o_ref[...] = diag

        def second_beside(g):
            if g < 8:
                rows = slice(g * 256, (g + 1) * 256)
                m_ref[local, rows, TILE:] = m_ref[local, rows, TILE:] - pair_product(rows)
            apply(unit_ref[p * SLOTS + 8 + g], old)
            if g >= 12:
                apply(unit_ref[p * SLOTS + 12 + g], old)

        invert_tile(a_ref, i_ref, s_ref, t_ref, second_beside)
        m_ref[local, tile_rows(k + 1), TILE:] = identity
        column(p, buf, 1)
        keep_own(k + 1, buf, 1)
        eh_ref[buf, tile_rows(k + 1), 0:TILE] = zero
        el_ref[buf, tile_rows(k + 1), 0:TILE] = zero
        wide = pl.ds(pl.multiple_of(local * 256, 256), 256)
        depth = last * 256
        xh_ref[:, wide] = eh_ref[buf, 0:depth, :]
        xl_ref[:, wide] = el_ref[buf, 0:depth, :]
        return carry

    lax.fori_loop(first, last, step, 0)
    if last < pairs:
        def flush(u, carry):
            apply(unit_ref[last * SLOTS + u], (last - 1) % 2)
            return carry

        lax.fori_loop(0, unit_ref[(pairs + 1) * SLOTS + last], flush, 0)
        next_ref[...] = m_ref[last - first : pairs - first]


def factor_stage(first, last, place, source):
    pairs = PANEL // 256
    vm = pl.BlockSpec(memory_space=pltpu.VMEM)
    smem = pl.BlockSpec(memory_space=pltpu.SMEM)
    wide = (last - first) * 256
    out_shape = [
        jax.ShapeDtypeStruct((2, TILE, TILE), jnp.bfloat16),
        jax.ShapeDtypeStruct((last * 256, wide), jnp.bfloat16),
        jax.ShapeDtypeStruct((last * 256, wide), jnp.bfloat16),
    ]
    if last < pairs:
        out_shape.append(jax.ShapeDtypeStruct((pairs - last, PANEL, 256), jnp.float32))
    tile = pltpu.VMEM((TILE, TILE), jnp.float32)
    return pl.pallas_call(
        functools.partial(factor_kernel, first, last),
        out_shape=tuple(out_shape),
        in_specs=[smem, smem, vm if first == 0 else pl.BlockSpec(memory_space=pl.ANY)],
        out_specs=tuple(vm for _ in out_shape),
        scratch_shapes=[
            pltpu.VMEM((pairs - first + 1, PANEL, 256), jnp.float32),
            pltpu.VMEM((2, PANEL, 256), jnp.bfloat16),
            pltpu.VMEM((2, PANEL, 256), jnp.bfloat16),
            tile,
            tile,
            tile,
            tile,
            tile,
            pltpu.SemaphoreType.DMA,
        ],
        compiler_params=pltpu.CompilerParams(vmem_limit_bytes=60 * 1024 * 1024),
        cost_estimate=pl.CostEstimate(flops=60_000_000_000, bytes_accessed=24_000_000, transcendentals=0),
        name="factor_corner",
    )(place, jnp.asarray(unit_table(first, last)), source)


def pack_kernel(slot_ref, child_ref, first_ref, second_ref):
    def move(t, carry):
        slot = slot_ref[t]

        @pl.when(slot % CAP == 0)
        def _():
            first_ref[slot // CAP] = child_ref[t]

        @pl.when(slot % CAP == 1)
        def _():
            second_ref[slot // CAP] = child_ref[t]

        return carry

    lax.fori_loop(0, child_ref.shape[0], move, 0)


def pack(slots, child_tiles):
    count = child_tiles.shape[0]
    vm = pl.BlockSpec(memory_space=pltpu.VMEM)
    return pl.pallas_call(
        pack_kernel,
        out_shape=tuple(jax.ShapeDtypeStruct((count, TILE, TILE), jnp.bfloat16) for _ in range(CAP)),
        in_specs=[pl.BlockSpec(memory_space=pltpu.SMEM), vm],
        out_specs=(vm, vm),
        compiler_params=pltpu.CompilerParams(vmem_limit_bytes=32 * 1024 * 1024),
        cost_estimate=pl.CostEstimate(flops=0, bytes_accessed=16_000_000, transcendentals=0),
        name="pack_tiles",
    )(slots, child_tiles)


def extend_kernel(id_ref, front_ref, first_ref, second_ref, after_ref, out_ref, panel_ref, acc_ref):
    cols_local = front_ref.shape[1] // TILE
    acc_ref[...] = front_ref[...].astype(jnp.float32)

    def add(s, carry):
        for part, tile_ref in enumerate((first_ref, second_ref)):
            local = id_ref[CAP * s + part]

            @pl.when(local >= 0)
            def _():
                rows = pl.ds(pl.multiple_of(local // cols_local * TILE, TILE), TILE)
                cols = pl.ds(pl.multiple_of(local % cols_local * TILE, TILE), TILE)
                acc_ref[rows, cols] = acc_ref[rows, cols] + tile_ref[s].astype(jnp.float32)

        return carry

    lax.fori_loop(0, first_ref.shape[0], add, 0)
    summed = acc_ref[...].astype(jnp.bfloat16)
    out_ref[...] = summed
    panel_ref[...] = summed[2 * TILE :, 0:TILE]


def extend(ids, front, first, second, after):
    vm = pl.BlockSpec(memory_space=pltpu.VMEM)
    return pl.pallas_call(
        extend_kernel,
        out_shape=(
            jax.ShapeDtypeStruct(front.shape, jnp.bfloat16),
            jax.ShapeDtypeStruct((front.shape[0] - 2 * TILE, TILE), jnp.bfloat16),
        ),
        in_specs=[pl.BlockSpec(memory_space=pltpu.SMEM), vm, vm, vm, pl.BlockSpec(memory_space=pl.ANY)],
        out_specs=(vm, vm),
        scratch_shapes=[pltpu.VMEM(front.shape, jnp.float32)],
        compiler_params=pltpu.CompilerParams(vmem_limit_bytes=48 * 1024 * 1024),
        cost_estimate=pl.CostEstimate(flops=10_000_000, bytes_accessed=30_000_000, transcendentals=0),
        name="extend_add",
    )(ids, front, first, second, after)


def finish_kernel(
    place_ref, xh1_ref, xl1_ref, xh2_ref, xl2_ref, row_ref, col_ref, own1_ref, own2_ref, assembled_ref, out_ref, a_ref, p_ref, acc_ref
):
    step = pl.program_id(0)
    steps = PANEL // (2 * TILE)
    rows_low = row_ref.shape[1] * TILE
    cols_low = col_ref.shape[1] * TILE
    total = rows_low + cols_low
    cols_local = assembled_ref.shape[1] // TILE
    c = place_ref[1]
    width = 2 * TILE

    @pl.when(step == 0)
    def _():
        top = 2 * TILE * cols_local
        out_ref[0:top, :] = jnp.zeros((top, TILE), jnp.float32)
        for a in range(2):
            rows = pl.ds(a * TILE * cols_local, TILE, stride=cols_local)
            out_ref[rows, :] = own1_ref[a].astype(jnp.float32) + own2_ref[a].astype(jnp.float32)
        acc_ref[...] = assembled_ref[2 * TILE :, TILE:].astype(jnp.float32)

    for s in range(steps):

        @pl.when(step == s)
        def _():
            for piece in range(2):
                lanes = slice(s * width + piece * TILE, s * width + (piece + 1) * TILE)
                a_ref[0:rows_low, lanes] = row_ref[piece].reshape(rows_low, TILE)
                a_ref[rows_low:total, lanes] = col_ref[piece].reshape(cols_low, TILE)
            depth = (s + 1) * width
            chunk = total
            xh_ref, xl_ref = (xh1_ref, xl1_ref) if s < steps // 2 else (xh2_ref, xl2_ref)

            def solve(b, carry):
                rows = pl.ds(pl.multiple_of(b * chunk, chunk), chunk)
                a = a_ref[rows, 0:depth]
                p = jnp.dot(a, xh_ref[0:depth, :], preferred_element_type=jnp.float32) + jnp.dot(
                    a, xl_ref[0:depth, :], preferred_element_type=jnp.float32
                )
                p_ref[rows, :] = p.astype(jnp.bfloat16)
                return carry

            lax.fori_loop(0, 1, solve, 0)

    @pl.when(step == c // 2)
    def _():
        lane = pl.multiple_of(c % 2 * TILE, TILE)
        rows = pl.ds(2 * TILE * cols_local, rows_low, stride=cols_local)
        out_ref[rows, :] = p_ref[0:rows_low, pl.ds(lane, TILE)].astype(jnp.float32)

    def update(b):
        rows = pl.ds(pl.multiple_of(b * 1792, 1792), 1792)
        return acc_ref[rows, :] - nt(p_ref[rows, :], p_ref[rows_low:total, :])

    def keep(b, carry):
        acc_ref[pl.ds(pl.multiple_of(b * 1792, 1792), 1792), :] = update(b)
        return carry

    def write(b, carry):
        u = update(b)
        for t in range(1, cols_local):
            target = pl.ds((b * 1792 + 2 * TILE) * cols_local + t, 1792, stride=cols_local)
            out_ref[target, :] = u[:, (t - 1) * TILE : t * TILE]
        return carry

    @pl.when(step < steps - 1)
    def _():
        lax.fori_loop(0, rows_low // 1792, keep, 0)

    @pl.when(step == steps - 1)
    def _():
        lax.fori_loop(0, rows_low // 1792, write, 0)


def finish(place, x1, x2, row_raw, col_raw, own1, own2, assembled):
    width = 2 * TILE
    steps = PANEL // width
    mid = steps // 2
    tiles_row = row_raw.shape[1]
    tiles_col = col_raw.shape[1]
    total = (tiles_row + tiles_col) * TILE
    vm = pl.BlockSpec(memory_space=pltpu.VMEM)
    early = pl.BlockSpec((PANEL // 2, width), lambda s: (0, jnp.minimum(s, mid - 1)))
    late = pl.BlockSpec((PANEL, width), lambda s: (0, jnp.maximum(s - mid, 0)))
    return pl.pallas_call(
        finish_kernel,
        grid=(steps,),
        out_shape=jax.ShapeDtypeStruct((assembled.shape[0] * assembled.shape[1] // TILE, TILE), jnp.float32),
        in_specs=[
            pl.BlockSpec(memory_space=pltpu.SMEM),
            early,
            early,
            late,
            late,
            pl.BlockSpec((2, tiles_row, TILE, TILE), lambda s: (s, 0, 0, 0)),
            pl.BlockSpec((2, tiles_col, TILE, TILE), lambda s: (s, 0, 0, 0)),
            vm,
            vm,
            vm,
        ],
        out_specs=vm,
        scratch_shapes=[
            pltpu.VMEM((total, PANEL), jnp.bfloat16),
            pltpu.VMEM((total, width), jnp.bfloat16),
            pltpu.VMEM((tiles_row * TILE, tiles_col * TILE), jnp.float32),
        ],
        compiler_params=pltpu.CompilerParams(
            vmem_limit_bytes=56 * 1024 * 1024, dimension_semantics=("arbitrary",)
        ),
        cost_estimate=pl.CostEstimate(flops=40_000_000_000, bytes_accessed=50_000_000, transcendentals=0),
        name="solve_update",
    )(place, *x1, *x2, row_raw, col_raw, own1, own2, assembled)


def per_device(front, child_tiles, tile_map):
    rows_local = front.shape[0]
    cols_local = front.shape[3]
    row_count = lax.axis_size("row")
    col_count = lax.axis_size("col")
    device_count = row_count * col_count
    row_index = lax.axis_index("row")
    col_index = lax.axis_index("col")
    both = ("row", "col")
    corner = front[0:2, 0, :, 0, 0, :]
    corner = lax.all_gather(corner, both, axis=0, tiled=False)

    owners = tile_map[:, 0] % row_count * col_count + tile_map[:, 1] % col_count
    local_ids = tile_map[:, 0] // row_count * cols_local + tile_map[:, 1] // col_count
    owner_hits = (owners[:, None] == jnp.arange(device_count)[None, :]).astype(jnp.int32)
    slot_rank = jnp.sum(jnp.cumsum(owner_hits, 0) * owner_hits, 1) - 1
    slot_index = owners * CAP + slot_rank
    def exchange(x):
        return lax.all_to_all(x, both, split_axis=0, concat_axis=0, tiled=True)

    first, second = pack(slot_index, child_tiles)
    targets = jnp.full((device_count * CAP,), -1, jnp.int32).at[slot_index].set(local_ids)
    arrived_ids = exchange(targets.reshape(device_count, CAP))
    first = exchange(first)
    flat_front = front.reshape(rows_local * TILE, cols_local * TILE)
    corner, second, flat_front = lax.optimization_barrier((corner, second, flat_front))
    second = exchange(second)

    place = jnp.stack([row_index, col_index]).astype(jnp.int32)
    own1, xh1, xl1, state = factor_stage(0, 4, place, corner)
    assembled, panel = extend(arrived_ids.reshape(device_count * CAP), flat_front, first, second, own1)
    low_tiles = rows_local - 2
    panel = panel.reshape(low_tiles, TILE, TILE)
    row_raw = lax.all_gather(panel, "col", axis=0, tiled=False)
    split_panel = panel.reshape(low_tiles // 2, 2, TILE, TILE)
    halves = (split_panel[:, 0], split_panel[:, 1])
    parity = col_index % 2
    received = []
    for k in range(2):
        pairs = []
        for r in range(row_count):
            for c in range(col_count):
                h = (c % 2) ^ k
                pairs.append((r * col_count + c, (c // 2) * col_count + row_count * h + r))
        outgoing = jnp.where(parity == k, halves[0], halves[1])
        received.append(lax.ppermute(outgoing, both, pairs))
    high = col_index // row_count
    first = jnp.where(high == 0, received[0], received[1])
    second = jnp.where(high == 0, received[1], received[0])
    pieces = jnp.broadcast_to(jnp.stack([first, second]), (row_count, 2) + first.shape)
    state, pieces = lax.optimization_barrier((state, pieces))
    col_raw = lax.all_to_all(
        pieces, "row", split_axis=0, concat_axis=0, tiled=True
    ).reshape(col_count, low_tiles // 2, TILE, TILE)
    own2, xh2, xl2 = factor_stage(4, 8, place, state)
    out = finish(place, (xh1, xl1), (xh2, xl2), row_raw, col_raw, own1, own2, assembled)
    return out.reshape(rows_local, 1, TILE, cols_local, 1, TILE)


def solution(mesh):
    in_specs = (
        P(None, "row", None, None, "col", None),
        P(("row", "col"), None, None),
        P(("row", "col"), None),
    )
    out_specs = P(None, "row", None, None, "col", None)
    return jax.shard_map(
        per_device, mesh=mesh, in_specs=in_specs, out_specs=out_specs, check_vma=False
    )
```

time: 543 us -> 376 us (0.69)
  the two profiles are of different devices: /device:TPU:1 before, /device:TPU:6 now
where the time goes in v2:
time: 376 us; the launch traced here: 371 us
  Pallas kernels  182 us (48%)
  waiting for transfers between devices  99.2 us (26%)
  starting transfers between devices  48.1 us (13%)
  local copies, waits for them, and re-layouts  21.3 us (6%)
  between operations  13.8 us (4%)
  other arithmetic  6.38 us (2%)
    pallas_call x2, Pallas kernels, factor_stage(): pl.pallas_call(functools.partial(factor_kernel, first, last), out_shape=t...  103 us
    all_gather x1, waiting for transfers between devices, per_device(): corner = lax.all_gather(corner, both, axis=0, tiled=False)  65.6 us
    pallas_call x1, Pallas kernels, finish(): pl.pallas_call(finish_kernel, grid=(steps,), out_shape=jax.ShapeDtypeStru...  65.1 us
    all_to_all x3, starting transfers between devices, exchange(): return lax.all_to_all(x, both, split_axis=0, concat_axis=0, tiled=True)  28.4 us
    ppermute x2, waiting for transfers between devices, per_device(): received.append(lax.ppermute(outgoing, both, pairs))  16.9 us
    all_to_all x1, waiting for transfers between devices, per_device(): lax.all_to_all(pieces, 'row', split_axis=0, concat_axis=0, tiled=True)  16.6 us
    unnamed x12, local copies, waits for them, and re-layouts  14.9 us
    all_to_all x1, starting transfers between devices, per_device(): lax.all_to_all(pieces, 'row', split_axis=0, concat_axis=0, tiled=True)  10.6 us
  transfers between devices with their start and end apart: 8, of which 4 were waited for; matrix products, arithmetic and copies ran while one was open for 4% of the time, Pallas kernels for 29%

profile of v2, /device:TPU:6, one launch (start us, length us, event | category | flops | bytes accessed | tf_op | source)
XLA Modules:
  0.0 371.0 jit_solution(10195965557546224979)
XLA Ops:
  6.5 1.1 slice.17
  7.7 0.6 copy.21
  8.3 0.8 fusion.11
  9.5 0.8 fusion.8
  10.3 0.8 multiply_add_fusion
  11.1 1.0 scatter_custom_fusion
  12.0 0.8 all_to_all.15
  12.8 10.5 %all-to-all-start = ((s32[128,1,2]{2,1,0:T(1,128)}), s32[128,1,2]{2,1,0:T(1,128)S(1)}, u32[]{:S(2)}, u32[]{:S(2)}) async-start(s32[128,1,2]{2,1,0:T(1,128)} %bitcast.8), calls=%async_computation | async-start | bytes 131072 | tf_op jit(solution)/shard_map/all_to_all | solution.py:493
  23.3 2.2 copy-done
  25.5 4.1 %pack_tiles.1 = (bf16[128,128,128]{2,1,0:T(8,128)(2,1)S(1)}, bf16[128,128,128]{2,1,0:T(8,128)(2,1)S(1)}) custom-call(s32[128]{0:T(128)S(1)} %get-tuple-element.40.slot_ref, bf16[128,128,128]{2,1,0:T(8,128)(2,1)S(1)} %copy-done), custom_call_target="tpu_custom_call" | custom-call | bytes 16000000 | tf_op jit(solution)/shard_map/pack_tiles/pallas_call | solution.py:311
  29.6 1.9 copy-done.1
  31.6 2.0 copy-done.2
  33.6 10.2 %all-to-all-start.1 = ((bf16[128,128,128]{2,1,0:T(8,128)(2,1)}), bf16[128,128,128]{2,1,0:T(8,128)(2,1)}, u32[]{:S(2)}, u32[]{:S(2)}) async-start(bf16[128,128,128]{2,1,0:T(8,128)(2,1)} %copy-done.2), calls=%async_computation.1 | async-start | bytes 8388608 | tf_op jit(solution)/shard_map/all_to_all | solution.py:493
  43.8 5.2 %copy.25 = bf16[256,8,8,128]{3,1,2,0:T(8,128)(2,1)} copy(bf16[256,8,8,128]{3,2,1,0:T(8,128)(2,1)} %bitcast.75) | data formatting | bytes 8388608
  50.2 0.8 reduce.3
  51.2 65.6 %all-gather.6.cloned.1.call-done = bf16[256,1,128,1,1,128]{5,2,4,3,1,0:T(8,128)(2,1)} async-done(((bf16[2,1,128,1,1,128]{5,2,4,3,1,0:T(8,128)(2,1)}), bf16[256,1,128,1,1,128]{5,2,4,3,1,0:T(8,128)(2,1)}) %all-gather.6.cloned.1.call-update) | async-done | bytes 8388624 | tf_op jit(solution)/shard_map/all_gather | solution.py:485
  116.8 7.7 %all-to-all-start.2 = ((bf16[128,128,128]{2,1,0:T(8,128)(2,1)}), bf16[128,128,128]{2,1,0:T(8,128)(2,1)}, u32[]{:S(2)}, u32[]{:S(2)}) async-start(bf16[128,128,128]{2,1,0:T(8,128)(2,1)} %copy-done.1), calls=%async_computation.2 | async-start | bytes 8388608 | tf_op jit(solution)/shard_map/all_to_all | solution.py:493
  124.7 56.0 %factor_corner.2 = (bf16[2,128,128]{2,1,0:T(8,128)(2,1)}, bf16[1024,1024]{1,0:T(8,128)(2,1)}, bf16[1024,1024]{1,0:T(8,128)(2,1)}, f32[4,2048,256]{2,1,0:T(8,128)}) custom-call(s32[2]{0:T(128)} %pad_add_fusion.place_ref, s32[585]{0:T(1024)} %constant.100.clone.unit_ref, bf16[128,2,128,128]{3,2,1,0:T(8,128)(2,1)} %bitcast.76), custom_call_target="tpu_custom_call" | custom-call | flops 60000002048 | bytes 24000000 | tf_op jit(solution)/shard_map/factor_corner/pallas_call | solution.py:269
  180.7 0.8 copy-done.3
  181.5 10.5 %extend_add.1 = (bf16[2048,1024]{1,0:T(8,128)(2,1)S(1)}, bf16[1792,128]{1,0:T(8,128)(2,1)}) custom-call(s32[256]{0:T(256)S(1)} %reshape.31.id_ref, bf16[2048,1024]{1,0:T(8,128)(2,1)} %bitcast.74, bf16[128,128,128]{2,1,0:T(8,128)(2,1)} %all-to-all-done.1.first_ref, bf16[128,128,128]{2,1,0:T(8,128)(2,1)} %all-to-all-done.2.second_ref, ...), custom_call_target="tpu_custom_call" | custom-call | flops 10000000 | bytes 30000000 | tf_op jit(solution)/shard_map/extend_add/pallas_call | solution.py:346
  192.0 2.1 copy-done.4
  194.1 1.1 select_bitcast_fusion.2
  195.2 4.0 %collective-permute-start.1 = (bf16[7,128,128]{2,1,0:T(8,128)(2,1)S(1)}, bf16[7,128,128]{2,1,0:T(8,128)(2,1)S(1)}, u32[]{:S(2)}, u32[]{:S(2)}) collective-permute-start(bf16[7,128,128]{2,1,0:T(8,128)(2,1)S(1)} %select_bitcast_fusion.2), channel_id=1, source_target_pairs={{0,8},{1,0},{2,24},{3,16},{4,40},{5,32},{6,56},{7,48},{8,72},{9,64... | collective-permute-start | bytes 688136 | tf_op jit(solution)/shard_map/ppermute | solution.py:520
  199.2 1.1 fusion
  200.3 4.8 %collective-permute-start = (bf16[7,128,128]{2,1,0:T(8,128)(2,1)S(1)}, bf16[7,128,128]{2,1,0:T(8,128)(2,1)S(1)}, u32[]{:S(2)}, u32[]{:S(2)}) collective-permute-start(bf16[7,128,128]{2,1,0:T(8,128)(2,1)S(1)} %fusion), channel_id=1, source_target_pairs={{0,0},{1,8},{2,16},{3,24},{4,32},{5,40},{6,48},{7,56},{8,64},{9,72... | collective-permute-start | bytes 688136 | tf_op jit(solution)/shard_map/ppermute | solution.py:520
  205.1 7.2 %collective-permute-done.1 = bf16[7,128,128]{2,1,0:T(8,128)(2,1)S(1)} collective-permute-done((bf16[7,128,128]{2,1,0:T(8,128)(2,1)S(1)}, bf16[7,128,128]{2,1,0:T(8,128)(2,1)S(1)}, u32[]{:S(2)}, u32[]{:S(2)}) %collective-permute-start.1) | collective-permute-done | bytes 229408 | tf_op jit(solution)/shard_map/ppermute | solution.py:520
  212.3 9.7 %collective-permute-done = bf16[7,128,128]{2,1,0:T(8,128)(2,1)S(1)} collective-permute-done((bf16[7,128,128]{2,1,0:T(8,128)(2,1)S(1)}, bf16[7,128,128]{2,1,0:T(8,128)(2,1)S(1)}, u32[]{:S(2)}, u32[]{:S(2)}) %collective-permute-start) | collective-permute-done | bytes 229408 | tf_op jit(solution)/shard_map/ppermute | solution.py:520
  222.2 2.8 broadcast_in_dim.10
  224.9 10.6 %all-to-all-start.3 = ((bf16[8,2,7,128,128]{4,3,2,1,0:T(8,128)(2,1)}), bf16[8,2,7,128,128]{4,3,2,1,0:T(8,128)(2,1)}, u32[]{:S(2)}, u32[]{:S(2)}) async-start(bf16[8,2,7,128,128]{4,3,2,1,0:T(8,128)(2,1)} %broadcast_in_dim.10), calls=%async_computation.3 | async-start | bytes 7340032 | tf_op jit(solution)/shard_map/all_to_all | solution.py:526
  235.6 46.6 %factor_corner.3 = (bf16[2,128,128]{2,1,0:T(8,128)(2,1)}, bf16[2048,1024]{1,0:T(8,128)(2,1)}, bf16[2048,1024]{1,0:T(8,128)(2,1)}) custom-call(s32[2]{0:T(128)} %pad_add_fusion.place_ref, s32[585]{0:T(1024)} %constant.101.clone.unit_ref, f32[4,2048,256]{2,1,0:T(8,128)} %get-tuple-element.31.source_ref), custom_call_target="tpu_custom_call" | custom-call | flops 60000002048 | bytes 24000000 | tf_op jit(solution)/shard_map/factor_corner/pallas_call | solution.py:269
  282.2 16.6 %all-to-all-done.3 = bf16[8,2,7,128,128]{4,3,2,1,0:T(8,128)(2,1)} async-done(((bf16[8,2,7,128,128]{4,3,2,1,0:T(8,128)(2,1)}), bf16[8,2,7,128,128]{4,3,2,1,0:T(8,128)(2,1)}, u32[]{:S(2)}, u32[]{:S(2)}) %all-to-all-start.3) | async-done | bytes 3670048 | tf_op jit(solution)/shard_map/all_to_all | solution.py:526
  298.8 65.1 %solve_update.1 = f32[16384,128]{1,0:T(8,128)} custom-call(s32[2]{0:T(128)} %pad_add_fusion.place_ref, bf16[1024,1024]{1,0:T(8,128)(2,1)} %get-tuple-element.23.xh1_ref, bf16[1024,1024]{1,0:T(8,128)(2,1)} %get-tuple-element.24.xl1_ref, bf16[2048,1024]{1,0:T(8,128)(2,1)} %get-tuple-element.32.xh2_ref, bf16[2048,1024]{1,0:T(8,128)(2,1)} %get-tuple-element.33.xl2_ref, ...), custom_call_target="tpu_custom_call" | custom-call | flops 40000000000 | bytes 50000000 | tf_op jit(solution)/shard_map/solve_update/pallas_call | solution.py:445
  (21 shorter events, 2.1 us)
Async XLA Ops:
  6.5 110.2 %all-gather.6.cloned.1.call-start = ((), (), s32[]{:S(2)}) async-start(), calls=%async_computation.5 | async-start | bytes 8454144 | tf_op jit(solution)/shard_map/all_gather | solution.py:485
  12.8 20.8 %all-to-all-start = ((s32[128,1,2]{2,1,0:T(1,128)}), s32[128,1,2]{2,1,0:T(1,128)S(1)}, u32[]{:S(2)}, u32[]{:S(2)}) async-start(s32[128,1,2]{2,1,0:T(1,128)} %bitcast.8), calls=%async_computation | async-start | bytes 131072 | tf_op jit(solution)/shard_map/all_to_all | solution.py:493
  23.3 2.2 copy-start
  29.6 1.9 copy-start.1
  31.6 2.0 copy-start.2
  33.6 83.2 %all-to-all-start.1 = ((bf16[128,128,128]{2,1,0:T(8,128)(2,1)}), bf16[128,128,128]{2,1,0:T(8,128)(2,1)}, u32[]{:S(2)}, u32[]{:S(2)}) async-start(bf16[128,128,128]{2,1,0:T(8,128)(2,1)} %copy-done.2), calls=%async_computation.1 | async-start | bytes 8388608 | tf_op jit(solution)/shard_map/all_to_all | solution.py:493
  116.8 63.9 %all-to-all-start.2 = ((bf16[128,128,128]{2,1,0:T(8,128)(2,1)}), bf16[128,128,128]{2,1,0:T(8,128)(2,1)}, u32[]{:S(2)}, u32[]{:S(2)}) async-start(bf16[128,128,128]{2,1,0:T(8,128)(2,1)} %copy-done.1), calls=%async_computation.2 | async-start | bytes 8388608 | tf_op jit(solution)/shard_map/all_to_all | solution.py:493
  124.5 174.3 %all-gather.4.cloned.1.call-start = ((), (), s32[]{:S(2)}) async-start(), calls=%async_computation.4 | async-start | bytes 7798784 | tf_op jit(solution)/shard_map/all_gather | solution.py:508
  180.7 0.8 copy-start.3
  192.0 2.1 copy-start.4
  195.2 17.1 %collective-permute-start.1 = (bf16[7,128,128]{2,1,0:T(8,128)(2,1)S(1)}, bf16[7,128,128]{2,1,0:T(8,128)(2,1)S(1)}, u32[]{:S(2)}, u32[]{:S(2)}) collective-permute-start(bf16[7,128,128]{2,1,0:T(8,128)(2,1)S(1)} %select_bitcast_fusion.2), channel_id=1, source_target_pairs={{0,8},{1,0},{2,24},{3,16},{4,40},{5,32},{6,56},{7,48},{8,72},{9,64... | collective-permute-start | bytes 688136 | tf_op jit(solution)/shard_map/ppermute | solution.py:520
  200.3 21.7 %collective-permute-start = (bf16[7,128,128]{2,1,0:T(8,128)(2,1)S(1)}, bf16[7,128,128]{2,1,0:T(8,128)(2,1)S(1)}, u32[]{:S(2)}, u32[]{:S(2)}) collective-permute-start(bf16[7,128,128]{2,1,0:T(8,128)(2,1)S(1)} %fusion), channel_id=1, source_target_pairs={{0,0},{1,8},{2,16},{3,24},{4,32},{5,40},{6,48},{7,56},{8,64},{9,72... | collective-permute-start | bytes 688136 | tf_op jit(solution)/shard_map/ppermute | solution.py:520
  224.9 73.9 %all-to-all-start.3 = ((bf16[8,2,7,128,128]{4,3,2,1,0:T(8,128)(2,1)}), bf16[8,2,7,128,128]{4,3,2,1,0:T(8,128)(2,1)}, u32[]{:S(2)}, u32[]{:S(2)}) async-start(bf16[8,2,7,128,128]{4,3,2,1,0:T(8,128)(2,1)} %broadcast_in_dim.10), calls=%async_computation.3 | async-start | bytes 7340032 | tf_op jit(solution)/shard_map/all_to_all | solution.py:526
Sparse Core Ops, SparseCore 0:
  10.3 106.3 all-gather.5
  194.3 66.5 all-gather.3

commit v3 on v2

--- a/solution.py
+++ b/solution.py
@@ -8,9 +8,11 @@
 from jax.sharding import PartitionSpec as P
 
 CAP = 2
+SPLIT = 2
 PANEL = 2048
 TILE = 128
 NT_DIMS = (((1,), (1,)), ((), ()))
+SLOTS = 32
 
 
 def split2(x):
@@ -91,29 +93,26 @@
 
 def unit_table(first, last):
     pairs = PANEL // 256
-    count = pairs - first
-    table = np.full((pairs + 1, 64), count * 8, np.int32)
-    lengths = np.zeros((pairs + 1,), np.int32)
-    for p in range(first, last + 1):
-        units = []
-        prev = p - 1
-        start = p + 1 if p < last else p
-        if prev >= first:
-            for q in range(start, pairs):
-                units += [(q - first) * 8 + b for b in range(pairs) if b <= prev or b >= q]
-        lengths[p] = len(units)
+    table = np.full((pairs, SLOTS), (pairs - first) * 8, np.int32)
+    for p in range(max(first, 1), last):
+        units = [(q - first) * 8 + b for q in range(p + 1, pairs) for b in range(pairs) if b <= p - 1 or b >= q]
         table[p, : len(units)] = units
-    return np.concatenate([table.reshape(-1), lengths])
-
-
-SLOTS = 64
-
-
-def factor_kernel(first, last, place_ref, unit_ref, source_ref, own_ref, xh_ref, xl_ref, *rest):
+    return table.reshape(-1)
+
+
+def factor_kernel(first, last, place_ref, unit_ref, *rest):
     tiles = PANEL // TILE
     pairs = tiles // 2
+    if first == 0:
+        source_ref, rest = rest[0], rest[1:]
+    else:
+        source_ref, oldh_ref, oldl_ref = rest[:3]
+        rest = rest[3:]
+    own_ref, xh_ref, xl_ref = rest[:3]
+    rest = rest[3:]
     if last < pairs:
-        next_ref, rest = rest[0], rest[1:]
+        next_ref, nexth_ref, nextl_ref = rest[:3]
+        rest = rest[3:]
     m_ref, eh_ref, el_ref, a_ref, o_ref, i_ref, s_ref, t_ref, sem = rest
     if first == 0:
         for j in range(tiles):
@@ -124,9 +123,15 @@
                 else:
                     m_ref[spot] = jnp.zeros((TILE, TILE), jnp.float32)
     else:
-        load = pltpu.make_async_copy(source_ref, m_ref.at[pl.ds(0, pairs - first)], sem)
-        load.start()
-        load.wait()
+        loads = (
+            pltpu.make_async_copy(source_ref, m_ref.at[pl.ds(0, pairs - first)], sem.at[0]),
+            pltpu.make_async_copy(oldh_ref, eh_ref.at[(first - 1) % 2], sem.at[1]),
+            pltpu.make_async_copy(oldl_ref, el_ref.at[(first - 1) % 2], sem.at[2]),
+        )
+        for load in loads:
+            load.start()
+        for load in loads:
+            load.wait()
     own_ref[...] = jnp.zeros_like(own_ref)
     r = place_ref[0]
     c = place_ref[1]
@@ -152,30 +157,31 @@
         cols = block_rows(jnp.minimum(q + first, pairs - 1))
         m_ref[q, rows, :] = m_ref[q, rows, :] - product(rows, cols, buf)
 
+    def times(x, y):
+        xh, xl = x
+        yh, yl = y
+        parts = nt(
+            jnp.concatenate([xh, xl], 1),
+            jnp.concatenate([jnp.concatenate([yh, yh], 1), jnp.concatenate([yl, yl], 1)], 0),
+        )
+        return parts[:, :TILE] + parts[:, TILE:]
+
     def keep_own(k, buf, half):
-        th, tl = split2(t_ref[...])
-        oh, ol = split2(o_ref[...])
-        both = jnp.concatenate([oh, ol], 1)
-        diag = nt(both, jnp.concatenate([th, th], 1)) + nt(both, jnp.concatenate([tl, tl], 1))
-        diag = jnp.where(row >= col, diag, 0.0).astype(jnp.bfloat16)
-
         @pl.when(k == c)
         def _():
+            diag = times(split2(o_ref[...]), split2(t_ref[...]))
+            diag = jnp.where(row >= col, diag, 0.0).astype(jnp.bfloat16)
             for a in range(2):
                 i = r + a * 8
                 src = eh_ref[buf, tile_rows(i), half * TILE : (half + 1) * TILE]
                 own_ref[a] = jnp.where(i == k, diag, jnp.where(i > k, src, zero))
 
     def column(p, buf, half):
-        th, tl = split2(t_ref[...])
-        tt1 = jnp.concatenate([th, th], 1)
-        tt2 = jnp.concatenate([tl, tl], 1)
+        inverse = split2(t_ref[...])
         lanes = slice(half * TILE, (half + 1) * TILE)
         for b in range(pairs):
             rows = slice(b * 256, (b + 1) * 256)
-            ch, cl = split2(m_ref[p - first, rows, lanes])
-            both = jnp.concatenate([ch, cl], 1)
-            eh, el = split2(nt(both, tt1) + nt(both, tt2))
+            eh, el = split2(times(split2(m_ref[p - first, rows, lanes]), inverse))
             eh_ref[buf, rows, lanes] = eh
             el_ref[buf, rows, lanes] = el
 
@@ -187,12 +193,7 @@
         m_ref[local, tile_rows(k), TILE:] = jnp.zeros((TILE, TILE), jnp.float32)
 
         diag = m_ref[local, tile_rows(k), 0:TILE]
-        if first == 0:
-            new = diag - product(tile_rows(k), tile_rows(k), old)
-            diag = jnp.where(p > first, new, diag)
-        else:
-            new = diag - product(tile_rows(k), tile_rows(k), old)
-            diag = jnp.where(p > first, new, diag)
+        diag = jnp.where(p > 0, diag - product(tile_rows(k), tile_rows(k), old), diag)
         a_ref[...] = diag
         o_ref[...] = diag
 
@@ -201,7 +202,7 @@
                 rows = slice(g * 256, (g + 1) * 256)
                 old_block = m_ref[local, rows, :]
                 new_block = old_block - product(rows, block_rows(p), old)
-                m_ref[local, rows, :] = jnp.where(p > first, new_block, old_block)
+                m_ref[local, rows, :] = jnp.where(p > 0, new_block, old_block)
             else:
                 apply(unit_ref[p * SLOTS + g - 8], old)
 
@@ -212,12 +213,11 @@
         keep_own(k, buf, 0)
 
         def pair_product(rows):
-            h = eh_ref[buf, rows, 0:TILE]
-            l = el_ref[buf, rows, 0:TILE]
-            fh = eh_ref[buf, tile_rows(k + 1), 0:TILE]
-            fl = el_ref[buf, tile_rows(k + 1), 0:TILE]
-            both = jnp.concatenate([h, l], 1)
-            return nt(both, jnp.concatenate([fh, fh], 1)) + nt(both, jnp.concatenate([fl, fl], 1))
+            lanes = slice(0, TILE)
+            return times(
+                (eh_ref[buf, rows, lanes], el_ref[buf, rows, lanes]),
+                (eh_ref[buf, tile_rows(k + 1), lanes], el_ref[buf, tile_rows(k + 1), lanes]),
+            )
 
         diag = m_ref[local, tile_rows(k + 1), TILE:] - pair_product(tile_rows(k + 1))
         a_ref[...] = diag
@@ -245,15 +245,12 @@
 
     lax.fori_loop(first, last, step, 0)
     if last < pairs:
-        def flush(u, carry):
-            apply(unit_ref[last * SLOTS + u], (last - 1) % 2)
-            return carry
-
-        lax.fori_loop(0, unit_ref[(pairs + 1) * SLOTS + last], flush, 0)
         next_ref[...] = m_ref[last - first : pairs - first]
-
-
-def factor_stage(first, last, place, source):
+        nexth_ref[...] = eh_ref[(last - 1) % 2]
+        nextl_ref[...] = el_ref[(last - 1) % 2]
+
+
+def factor_stage(first, last, place, *sources):
     pairs = PANEL // 256
     vm = pl.BlockSpec(memory_space=pltpu.VMEM)
     smem = pl.BlockSpec(memory_space=pltpu.SMEM)
@@ -265,11 +262,12 @@
     ]
     if last < pairs:
         out_shape.append(jax.ShapeDtypeStruct((pairs - last, PANEL, 256), jnp.float32))
+        out_shape += [jax.ShapeDtypeStruct((PANEL, 256), jnp.bfloat16)] * 2
     tile = pltpu.VMEM((TILE, TILE), jnp.float32)
     return pl.pallas_call(
         functools.partial(factor_kernel, first, last),
         out_shape=tuple(out_shape),
-        in_specs=[smem, smem, vm if first == 0 else pl.BlockSpec(memory_space=pl.ANY)],
+        in_specs=[smem, smem] + ([vm] if first == 0 else [pl.BlockSpec(memory_space=pl.ANY)] * 3),
         out_specs=tuple(vm for _ in out_shape),
         scratch_shapes=[
             pltpu.VMEM((pairs - first + 1, PANEL, 256), jnp.float32),
@@ -280,26 +278,17 @@
             tile,
             tile,
             tile,
-            pltpu.SemaphoreType.DMA,
+            pltpu.SemaphoreType.DMA((3,)),
         ],
         compiler_params=pltpu.CompilerParams(vmem_limit_bytes=60 * 1024 * 1024),
         cost_estimate=pl.CostEstimate(flops=60_000_000_000, bytes_accessed=24_000_000, transcendentals=0),
         name="factor_corner",
-    )(place, jnp.asarray(unit_table(first, last)), source)
-
-
-def pack_kernel(slot_ref, child_ref, first_ref, second_ref):
+    )(place, jnp.asarray(unit_table(first, last)), *sources)
+
+
+def pack_kernel(slot_ref, child_ref, packed_ref):
     def move(t, carry):
-        slot = slot_ref[t]
-
-        @pl.when(slot % CAP == 0)
-        def _():
-            first_ref[slot // CAP] = child_ref[t]
-
-        @pl.when(slot % CAP == 1)
-        def _():
-            second_ref[slot // CAP] = child_ref[t]
-
+        packed_ref[slot_ref[t]] = child_ref[t]
         return carry
 
     lax.fori_loop(0, child_ref.shape[0], move, 0)
@@ -310,38 +299,37 @@
     vm = pl.BlockSpec(memory_space=pltpu.VMEM)
     return pl.pallas_call(
         pack_kernel,
-        out_shape=tuple(jax.ShapeDtypeStruct((count, TILE, TILE), jnp.bfloat16) for _ in range(CAP)),
+        out_shape=jax.ShapeDtypeStruct((CAP * count, TILE, TILE), jnp.bfloat16),
         in_specs=[pl.BlockSpec(memory_space=pltpu.SMEM), vm],
-        out_specs=(vm, vm),
+        out_specs=vm,
         compiler_params=pltpu.CompilerParams(vmem_limit_bytes=32 * 1024 * 1024),
         cost_estimate=pl.CostEstimate(flops=0, bytes_accessed=16_000_000, transcendentals=0),
         name="pack_tiles",
     )(slots, child_tiles)
 
 
-def extend_kernel(id_ref, front_ref, first_ref, second_ref, after_ref, out_ref, panel_ref, acc_ref):
+def extend_kernel(id_ref, front_ref, arrived_ref, out_ref, panel_ref, acc_ref):
     cols_local = front_ref.shape[1] // TILE
     acc_ref[...] = front_ref[...].astype(jnp.float32)
 
     def add(s, carry):
-        for part, tile_ref in enumerate((first_ref, second_ref)):
-            local = id_ref[CAP * s + part]
-
-            @pl.when(local >= 0)
-            def _():
-                rows = pl.ds(pl.multiple_of(local // cols_local * TILE, TILE), TILE)
-                cols = pl.ds(pl.multiple_of(local % cols_local * TILE, TILE), TILE)
-                acc_ref[rows, cols] = acc_ref[rows, cols] + tile_ref[s].astype(jnp.float32)
+        local = id_ref[s]
+
+        @pl.when(local >= 0)
+        def _():
+            rows = pl.ds(pl.multiple_of(local // cols_local * TILE, TILE), TILE)
+            cols = pl.ds(pl.multiple_of(local % cols_local * TILE, TILE), TILE)
+            acc_ref[rows, cols] = acc_ref[rows, cols] + arrived_ref[s].astype(jnp.float32)
 
         return carry
 
-    lax.fori_loop(0, first_ref.shape[0], add, 0)
+    lax.fori_loop(0, arrived_ref.shape[0], add, 0)
     summed = acc_ref[...].astype(jnp.bfloat16)
     out_ref[...] = summed
     panel_ref[...] = summed[2 * TILE :, 0:TILE]
 
 
-def extend(ids, front, first, second, after):
+def extend(ids, front, arrived):
     vm = pl.BlockSpec(memory_space=pltpu.VMEM)
     return pl.pallas_call(
         extend_kernel,
@@ -349,17 +337,17 @@
             jax.ShapeDtypeStruct(front.shape, jnp.bfloat16),
             jax.ShapeDtypeStruct((front.shape[0] - 2 * TILE, TILE), jnp.bfloat16),
         ),
-        in_specs=[pl.BlockSpec(memory_space=pltpu.SMEM), vm, vm, vm, pl.BlockSpec(memory_space=pl.ANY)],
+        in_specs=[pl.BlockSpec(memory_space=pltpu.SMEM), vm, vm],
         out_specs=(vm, vm),
         scratch_shapes=[pltpu.VMEM(front.shape, jnp.float32)],
         compiler_params=pltpu.CompilerParams(vmem_limit_bytes=48 * 1024 * 1024),
         cost_estimate=pl.CostEstimate(flops=10_000_000, bytes_accessed=30_000_000, transcendentals=0),
         name="extend_add",
-    )(ids, front, first, second, after)
+    )(ids, front, arrived)
 
 
 def finish_kernel(
-    place_ref, xh1_ref, xl1_ref, xh2_ref, xl2_ref, row_ref, col_ref, own1_ref, own2_ref, assembled_ref, out_ref, a_ref, p_ref, acc_ref
+    place_ref, xh1_ref, xl1_ref, xh2_ref, xl2_ref, row_ref, col_ref, own1_ref, own2_ref, assembled_ref, out_ref, a_ref, p_ref, sum_ref, acc_ref
 ):
     step = pl.program_id(0)
     steps = PANEL // (2 * TILE)
@@ -379,28 +367,36 @@
             out_ref[rows, :] = own1_ref[a].astype(jnp.float32) + own2_ref[a].astype(jnp.float32)
         acc_ref[...] = assembled_ref[2 * TILE :, TILE:].astype(jnp.float32)
 
-    for s in range(steps):
-
-        @pl.when(step == s)
-        def _():
-            for piece in range(2):
-                lanes = slice(s * width + piece * TILE, s * width + (piece + 1) * TILE)
-                a_ref[0:rows_low, lanes] = row_ref[piece].reshape(rows_low, TILE)
-                a_ref[rows_low:total, lanes] = col_ref[piece].reshape(cols_low, TILE)
-            depth = (s + 1) * width
-            chunk = total
-            xh_ref, xl_ref = (xh1_ref, xl1_ref) if s < steps // 2 else (xh2_ref, xl2_ref)
-
-            def solve(b, carry):
-                rows = pl.ds(pl.multiple_of(b * chunk, chunk), chunk)
-                a = a_ref[rows, 0:depth]
-                p = jnp.dot(a, xh_ref[0:depth, :], preferred_element_type=jnp.float32) + jnp.dot(
-                    a, xl_ref[0:depth, :], preferred_element_type=jnp.float32
-                )
-                p_ref[rows, :] = p.astype(jnp.bfloat16)
-                return carry
-
-            lax.fori_loop(0, 1, solve, 0)
+    for piece in range(2):
+        lanes = slice(piece * TILE, (piece + 1) * TILE)
+        a_ref[step, 0:rows_low, lanes] = row_ref[piece].reshape(rows_low, TILE)
+        a_ref[step, rows_low:total, lanes] = col_ref[piece].reshape(cols_low, TILE)
+
+    def solve_with(xh_ref, xl_ref):
+        def part(kk):
+            rows = pl.ds(pl.multiple_of(kk * width, width), width)
+            a = a_ref[kk]
+            return jnp.dot(a, xh_ref[rows, :], preferred_element_type=jnp.float32) + jnp.dot(
+                a, xl_ref[rows, :], preferred_element_type=jnp.float32
+            )
+
+        def solve(kk, carry):
+            sum_ref[...] = sum_ref[...] + part(kk)
+            return carry
+
+        sum_ref[...] = jnp.zeros_like(sum_ref)
+        lax.fori_loop(0, step, solve, 0)
+        p_ref[...] = (sum_ref[...] + part(step)).astype(jnp.bfloat16)
+
+    mid = xh1_ref.shape[0] // width
+
+    @pl.when(step < mid)
+    def _():
+        solve_with(xh1_ref, xl1_ref)
+
+    @pl.when(step >= mid)
+    def _():
+        solve_with(xh2_ref, xl2_ref)
 
     @pl.when(step == c // 2)
     def _():
@@ -408,39 +404,33 @@
         rows = pl.ds(2 * TILE * cols_local, rows_low, stride=cols_local)
         out_ref[rows, :] = p_ref[0:rows_low, pl.ds(lane, TILE)].astype(jnp.float32)
 
-    def update(b):
-        rows = pl.ds(pl.multiple_of(b * 1792, 1792), 1792)
-        return acc_ref[rows, :] - nt(p_ref[rows, :], p_ref[rows_low:total, :])
-
-    def keep(b, carry):
-        acc_ref[pl.ds(pl.multiple_of(b * 1792, 1792), 1792), :] = update(b)
+    def update(b, carry):
+        rows = pl.ds(pl.multiple_of(b * chunk, chunk), chunk)
+        acc_ref[rows, :] = acc_ref[rows, :] - nt(p_ref[rows, :], p_ref[rows_low:total, :])
         return carry
 
-    def write(b, carry):
-        u = update(b)
-        for t in range(1, cols_local):
-            target = pl.ds((b * 1792 + 2 * TILE) * cols_local + t, 1792, stride=cols_local)
-            out_ref[target, :] = u[:, (t - 1) * TILE : t * TILE]
-        return carry
-
-    @pl.when(step < steps - 1)
-    def _():
-        lax.fori_loop(0, rows_low // 1792, keep, 0)
+    chunk = rows_low
+    lax.fori_loop(0, 1, update, 0)
 
     @pl.when(step == steps - 1)
     def _():
-        lax.fori_loop(0, rows_low // 1792, write, 0)
+        def write(t, carry):
+            lanes = pl.ds(pl.multiple_of((t - 1) * TILE, TILE), TILE)
+            out_ref[pl.ds(2 * TILE * cols_local + t, rows_low, stride=cols_local), :] = acc_ref[:, lanes]
+            return carry
+
+        lax.fori_loop(1, cols_local, write, 0)
 
 
 def finish(place, x1, x2, row_raw, col_raw, own1, own2, assembled):
     width = 2 * TILE
     steps = PANEL // width
-    mid = steps // 2
+    mid = x1[0].shape[1] // width
     tiles_row = row_raw.shape[1]
     tiles_col = col_raw.shape[1]
     total = (tiles_row + tiles_col) * TILE
     vm = pl.BlockSpec(memory_space=pltpu.VMEM)
-    early = pl.BlockSpec((PANEL // 2, width), lambda s: (0, jnp.minimum(s, mid - 1)))
+    early = pl.BlockSpec((mid * width, width), lambda s: (0, jnp.minimum(s, mid - 1)))
     late = pl.BlockSpec((PANEL, width), lambda s: (0, jnp.maximum(s - mid, 0)))
     return pl.pallas_call(
         finish_kernel,
@@ -460,8 +450,9 @@
         ],
         out_specs=vm,
         scratch_shapes=[
-            pltpu.VMEM((total, PANEL), jnp.bfloat16),
+            pltpu.VMEM((steps, total, width), jnp.bfloat16),
             pltpu.VMEM((total, width), jnp.bfloat16),
+            pltpu.VMEM((total, width), jnp.float32),
             pltpu.VMEM((tiles_row * TILE, tiles_col * TILE), jnp.float32),
         ],
         compiler_params=pltpu.CompilerParams(
@@ -489,20 +480,21 @@
     owner_hits = (owners[:, None] == jnp.arange(device_count)[None, :]).astype(jnp.int32)
     slot_rank = jnp.sum(jnp.cumsum(owner_hits, 0) * owner_hits, 1) - 1
     slot_index = owners * CAP + slot_rank
+
     def exchange(x):
-        return lax.all_to_all(x, both, split_axis=0, concat_axis=0, tiled=True)
-
-    first, second = pack(slot_index, child_tiles)
+        return lax.all_to_all(
+            x.reshape((device_count, CAP) + x.shape[1:]), both, split_axis=0, concat_axis=0, tiled=True
+        ).reshape(x.shape)
+
     targets = jnp.full((device_count * CAP,), -1, jnp.int32).at[slot_index].set(local_ids)
-    arrived_ids = exchange(targets.reshape(device_count, CAP))
-    first = exchange(first)
+    arrived = exchange(pack(slot_index, child_tiles))
     flat_front = front.reshape(rows_local * TILE, cols_local * TILE)
-    corner, second, flat_front = lax.optimization_barrier((corner, second, flat_front))
-    second = exchange(second)
+    targets, flat_front = lax.optimization_barrier((targets, flat_front))
+    assembled, panel = extend(exchange(targets), flat_front, arrived)
+    corner, panel = lax.optimization_barrier((corner, panel))
 
     place = jnp.stack([row_index, col_index]).astype(jnp.int32)
-    own1, xh1, xl1, state = factor_stage(0, 4, place, corner)
-    assembled, panel = extend(arrived_ids.reshape(device_count * CAP), flat_front, first, second, own1)
+    own1, xh1, xl1, *state = factor_stage(0, SPLIT, place, corner)
     low_tiles = rows_local - 2
     panel = panel.reshape(low_tiles, TILE, TILE)
     row_raw = lax.all_gather(panel, "col", axis=0, tiled=False)
@@ -522,11 +514,11 @@
     first = jnp.where(high == 0, received[0], received[1])
     second = jnp.where(high == 0, received[1], received[0])
     pieces = jnp.broadcast_to(jnp.stack([first, second]), (row_count, 2) + first.shape)
-    state, pieces = lax.optimization_barrier((state, pieces))
+    *state, pieces = lax.optimization_barrier((*state, pieces))
     col_raw = lax.all_to_all(
         pieces, "row", split_axis=0, concat_axis=0, tiled=True
     ).reshape(col_count, low_tiles // 2, TILE, TILE)
-    own2, xh2, xl2 = factor_stage(4, 8, place, state)
+    own2, xh2, xl2 = factor_stage(SPLIT, PANEL // 256, place, *state)
     out = finish(place, (xh1, xl1), (xh2, xl2), row_raw, col_raw, own1, own2, assembled)
     return out.reshape(rows_local, 1, TILE, cols_local, 1, TILE)
 

time: 376 us -> 353 us (0.939)
  the two profiles are of different devices: /device:TPU:6 before, /device:TPU:1 now
where the time goes in v3:
time: 353 us; the launch traced here: 350 us
  Pallas kernels  161 us (46%)
  waiting for transfers between devices  111 us (31%)
  starting transfers between devices  40.3 us (11%)
  local copies, waits for them, and re-layouts  19.8 us (6%)
  between operations  13.6 us (4%)
  other arithmetic  4.15 us (1%)
    all_to_all x2, waiting for transfers between devices, exchange(): lax.all_to_all(x.reshape((device_count, CAP) + x.shape[1:]), both, split_...  111 us
    pallas_call x2, Pallas kernels, factor_stage(): pl.pallas_call(functools.partial(factor_kernel, first, last), out_shape=t...  94.9 us
    pallas_call x1, Pallas kernels, finish(): pl.pallas_call(finish_kernel, grid=(steps,), out_shape=jax.ShapeDtypeStru...  54.6 us
    all_to_all x2, starting transfers between devices, exchange(): lax.all_to_all(x.reshape((device_count, CAP) + x.shape[1:]), both, split_...  19.1 us
    all_to_all x1, starting transfers between devices, per_device(): lax.all_to_all(pieces, 'row', split_axis=0, concat_axis=0, tiled=True)  16.7 us
    unnamed x10, local copies, waits for them, and re-layouts  13.5 us
    pallas_call x1, Pallas kernels, extend(): pl.pallas_call(extend_kernel, out_shape=(jax.ShapeDtypeStruct(front.shape...  10 us
  transfers between devices with their start and end apart: 7, of which 2 were waited for; matrix products, arithmetic and copies ran while one was open for 4% of the time, Pallas kernels for 30%

profile of v3, /device:TPU:1, one launch (start us, length us, event | category | flops | bytes accessed | tf_op | source)
XLA Modules:
  0.0 349.6 jit_solution(9620297689628955062)
XLA Ops:
  6.5 1.1 slice.17
  7.7 0.6 copy.21
  8.3 5.2 %copy.25 = bf16[256,8,8,128]{3,1,2,0:T(8,128)(2,1)} copy(bf16[256,8,8,128]{3,2,1,0:T(8,128)(2,1)} %bitcast.78) | data formatting | bytes 8388608
  13.6 0.1 fusion.1
  13.7 0.2 reduce_window_sum.11
  13.8 0.2 select_reduce_fusion
  14.1 1.0 scatter_custom_fusion
  15.0 0.8 all_to_all.12
  15.8 11.5 %all-to-all-start = ((s32[128,1,2]{2,1,0:T(1,128)}), s32[128,1,2]{2,1,0:T(1,128)S(1)}, u32[]{:S(2)}, u32[]{:S(2)}) async-start(s32[128,1,2]{2,1,0:T(1,128)} %bitcast.8), calls=%async_computation | async-start | bytes 131072 | tf_op jit(solution)/shard_map/all_to_all | solution.py:485
  27.3 2.2 copy-done.1
  29.5 1.3 pack_tiles.1
  30.9 3.4 copy-done
  34.3 2.7 all-to-all-done
  36.9 7.6 %all-to-all-start.1 = ((bf16[128,2,128,128]{3,2,1,0:T(8,128)(2,1)}), bf16[128,2,128,128]{3,2,1,0:T(8,128)(2,1)}, u32[]{:S(2)}, u32[]{:S(2)}) async-start(bf16[128,2,128,128]{3,2,1,0:T(8,128)(2,1)} %bitcast.76), calls=%async_computation.1 | async-start | bytes 16777216 | tf_op jit(solution)/shard_map/all_to_all | solution.py:485
  44.5 0.0 all-gather.4.cloned.1.call-start
  44.6 0.6 broadcast.102
  45.1 0.8 reduce.3
  46.0 0.1 reshape.37.id_ref
  46.1 108.1 %all-to-all-done.1 = bf16[128,2,128,128]{3,2,1,0:T(8,128)(2,1)} async-done(((bf16[128,2,128,128]{3,2,1,0:T(8,128)(2,1)}), bf16[128,2,128,128]{3,2,1,0:T(8,128)(2,1)}, u32[]{:S(2)}, u32[]{:S(2)}) %all-to-all-start.1) | async-done | bytes 8388640 | tf_op jit(solution)/shard_map/all_to_all | solution.py:485
  154.2 10.0 %extend_add.1 = (bf16[2048,1024]{1,0:T(8,128)(2,1)S(1)}, bf16[1792,128]{1,0:T(8,128)(2,1)}) custom-call(s32[256]{0:T(256)S(1)} %reshape.37.id_ref, bf16[2048,1024]{1,0:T(8,128)(2,1)} %bitcast.77, bf16[256,128,128]{2,1,0:T(8,128)(2,1)} %bitcast.10.arrived_ref), custom_call_target="tpu_custom_call" | custom-call | flops 10000000 | bytes 30000000 | tf_op jit(solution)/shard_map/extend_add/pallas_call | solution.py:334
  164.3 2.1 copy-done.2
  166.4 0.6 pad_add_fusion.place_ref
  167.0 1.1 fusion
  168.1 1.9 collective-permute-start
  170.0 1.1 select_bitcast_fusion.2
  171.1 2.6 collective-permute-start.1
  173.7 28.9 %factor_corner.2 = (bf16[2,128,128]{2,1,0:T(8,128)(2,1)}, bf16[512,512]{1,0:T(8,128)(2,1)}, bf16[512,512]{1,0:T(8,128)(2,1)}, f32[6,2048,256]{2,1,0:T(8,128)}, b...) custom-call(s32[2]{0:T(128)} %pad_add_fusion.place_ref, s32[256]{0:T(256)} %constant.100.clone.unit_ref, ...), custom_call_target="tpu_custom_call" | custom-call | flops 60000002048 | bytes 24000000 | tf_op jit(solution)/shard_map/factor_corner/pallas_call | solution.py:267
  202.7 2.7 broadcast_in_dim.10
  205.5 16.7 %all-to-all-start.2 = ((bf16[8,2,7,128,128]{4,3,2,1,0:T(8,128)(2,1)}), bf16[8,2,7,128,128]{4,3,2,1,0:T(8,128)(2,1)}, u32[]{:S(2)}, u32[]{:S(2)}) async-start(bf16[8,2,7,128,128]{4,3,2,1,0:T(8,128)(2,1)} %broadcast_in_dim.10), calls=%async_computation.2 | async-start | bytes 7340032 | tf_op jit(solution)/shard_map/all_to_all | solution.py:518
  222.2 66.0 %factor_corner.3 = (bf16[2,128,128]{2,1,0:T(8,128)(2,1)}, bf16[2048,1536]{1,0:T(8,128)(2,1)}, bf16[2048,1536]{1,0:T(8,128)(2,1)}) custom-call(s32[2]{0:T(128)} %pad_add_fusion.place_ref, s32[256]{0:T(256)} %constant.101.clone.unit_ref, f32[6,2048,256]{2,1,0:T(8,128)} %get-tuple-element.34.rest_0_, bf16[2048,256]{1,0:T(8,128)(2,1)} %get-tuple-element.35.rest_1_, ...), custom_call_target="tpu_custom_call" | custom-call | flops 60000002048 | bytes 24000000 | tf_op jit(solution)/shard_map/factor_corner/pallas_call | solution.py:267
  288.2 0.0 all-gather.4.cloned.1.call-done.row_ref
  288.2 54.6 %solve_update.1 = f32[16384,128]{1,0:T(8,128)} custom-call(s32[2]{0:T(128)} %pad_add_fusion.place_ref, bf16[512,512]{1,0:T(8,128)(2,1)} %get-tuple-element.28.xh1_ref, bf16[512,512]{1,0:T(8,128)(2,1)} %get-tuple-element.29.xl1_ref, bf16[2048,1536]{1,0:T(8,128)(2,1)} %get-tuple-element.37.xh2_ref, bf16[2048,1536]{1,0:T(8,128)(2,1)} %get-tuple-element.38.xl2_ref, ...), custom_call_target="tpu_custom_call" | custom-call | flops 40000000000 | bytes 50000000 | tf_op jit(solution)/shard_map/solve_update/pallas_call | solution.py:435
  (17 shorter events, 0.2 us)
Async XLA Ops:
  6.5 7.0 %copy-start.3 = (s32[128,2]{0,1:T(2,128)S(1)}, s32[128,2]{0,1:T(2,128)}, u32[]{:S(2)}) copy-start(s32[128,2]{0,1:T(2,128)} %param.7) | copy-start | bytes 3076
  6.5 159.8 %all-gather.6.cloned.1.call-start = ((), (), s32[]{:S(2)}) async-start(), calls=%async_computation.4 | async-start | bytes 8454144 | tf_op jit(solution)/shard_map/all_gather | solution.py:476
  15.8 21.1 %all-to-all-start = ((s32[128,1,2]{2,1,0:T(1,128)}), s32[128,1,2]{2,1,0:T(1,128)S(1)}, u32[]{:S(2)}, u32[]{:S(2)}) async-start(s32[128,1,2]{2,1,0:T(1,128)} %bitcast.8), calls=%async_computation | async-start | bytes 131072 | tf_op jit(solution)/shard_map/all_to_all | solution.py:485
  27.3 2.2 copy-start.1
  30.9 3.4 copy-start
  36.9 117.3 %all-to-all-start.1 = ((bf16[128,2,128,128]{3,2,1,0:T(8,128)(2,1)}), bf16[128,2,128,128]{3,2,1,0:T(8,128)(2,1)}, u32[]{:S(2)}, u32[]{:S(2)}) async-start(bf16[128,2,128,128]{3,2,1,0:T(8,128)(2,1)} %bitcast.76), calls=%async_computation.1 | async-start | bytes 16777216 | tf_op jit(solution)/shard_map/all_to_all | solution.py:485
  44.5 243.7 %all-gather.4.cloned.1.call-start = ((), (), s32[]{:S(2)}) async-start(), calls=%async_computation.3 | async-start | bytes 7798784 | tf_op jit(solution)/shard_map/all_gather | solution.py:500
  164.3 2.1 copy-start.2
  168.1 34.5 %collective-permute-start = (bf16[7,128,128]{2,1,0:T(8,128)(2,1)S(1)}, bf16[7,128,128]{2,1,0:T(8,128)(2,1)S(1)}, u32[]{:S(2)}, u32[]{:S(2)}) collective-permute-start(bf16[7,128,128]{2,1,0:T(8,128)(2,1)S(1)} %fusion), channel_id=1, source_target_pairs={{0,0},{1,8},{2,16},{3,24},{4,32},{5,40},{6,48},{7,56},{8,64},{9,72... | collective-permute-start | bytes 688136 | tf_op jit(solution)/shard_map/ppermute | solution.py:512
  171.1 31.5 %collective-permute-start.1 = (bf16[7,128,128]{2,1,0:T(8,128)(2,1)S(1)}, bf16[7,128,128]{2,1,0:T(8,128)(2,1)S(1)}, u32[]{:S(2)}, u32[]{:S(2)}) collective-permute-start(bf16[7,128,128]{2,1,0:T(8,128)(2,1)S(1)} %select_bitcast_fusion.2), channel_id=1, source_target_pairs={{0,8},{1,0},{2,24},{3,16},{4,40},{5,32},{6,56},{7,48},{8,72},{9,64... | collective-permute-start | bytes 688136 | tf_op jit(solution)/shard_map/ppermute | solution.py:512
  205.5 82.7 %all-to-all-start.2 = ((bf16[8,2,7,128,128]{4,3,2,1,0:T(8,128)(2,1)}), bf16[8,2,7,128,128]{4,3,2,1,0:T(8,128)(2,1)}, u32[]{:S(2)}, u32[]{:S(2)}) async-start(bf16[8,2,7,128,128]{4,3,2,1,0:T(8,128)(2,1)} %broadcast_in_dim.10), calls=%async_computation.2 | async-start | bytes 7340032 | tf_op jit(solution)/shard_map/all_to_all | solution.py:518
Sparse Core Ops, SparseCore 0:
  10.3 149.4 all-gather.5
  166.5 87.5 all-gather.3

commit v4 on v3

--- a/solution.py
+++ b/solution.py
@@ -8,6 +8,7 @@
 from jax.sharding import PartitionSpec as P
 
 CAP = 2
+HEAD = 16
 SPLIT = 2
 PANEL = 2048
 TILE = 128
@@ -286,45 +287,48 @@
     )(place, jnp.asarray(unit_table(first, last)), *sources)
 
 
-def pack_kernel(slot_ref, child_ref, packed_ref):
+def pack_kernel(slot_ref, child_ref, head_ref, packed_ref):
+    packed_ref[:, CAP * TILE :, :] = head_ref[...]
+
     def move(t, carry):
-        packed_ref[slot_ref[t]] = child_ref[t]
+        slot = slot_ref[t]
+        rows = pl.ds(pl.multiple_of(slot % CAP * TILE, TILE), TILE)
+        packed_ref[slot // CAP, rows, :] = child_ref[t]
         return carry
 
     lax.fori_loop(0, child_ref.shape[0], move, 0)
 
 
-def pack(slots, child_tiles):
-    count = child_tiles.shape[0]
+def pack(slots, child_tiles, head):
     vm = pl.BlockSpec(memory_space=pltpu.VMEM)
     return pl.pallas_call(
         pack_kernel,
-        out_shape=jax.ShapeDtypeStruct((CAP * count, TILE, TILE), jnp.bfloat16),
-        in_specs=[pl.BlockSpec(memory_space=pltpu.SMEM), vm],
+        out_shape=jax.ShapeDtypeStruct((head.shape[0], CAP * TILE + HEAD, TILE), jnp.bfloat16),
+        in_specs=[pl.BlockSpec(memory_space=pltpu.SMEM), vm, vm],
         out_specs=vm,
         compiler_params=pltpu.CompilerParams(vmem_limit_bytes=32 * 1024 * 1024),
         cost_estimate=pl.CostEstimate(flops=0, bytes_accessed=16_000_000, transcendentals=0),
         name="pack_tiles",
-    )(slots, child_tiles)
+    )(slots, child_tiles, head)
 
 
 def extend_kernel(id_ref, front_ref, arrived_ref, out_ref, panel_ref, acc_ref):
     cols_local = front_ref.shape[1] // TILE
-    acc_ref[...] = front_ref[...].astype(jnp.float32)
+    rows_local = front_ref.shape[0]
+    acc_ref[0:rows_local, :] = front_ref[...].astype(jnp.float32)
 
     def add(s, carry):
         local = id_ref[s]
-
-        @pl.when(local >= 0)
-        def _():
-            rows = pl.ds(pl.multiple_of(local // cols_local * TILE, TILE), TILE)
-            cols = pl.ds(pl.multiple_of(local % cols_local * TILE, TILE), TILE)
-            acc_ref[rows, cols] = acc_ref[rows, cols] + arrived_ref[s].astype(jnp.float32)
-
+        used = local >= 0
+        top = jnp.where(used, local // cols_local * TILE, rows_local)
+        left = jnp.where(used, local % cols_local * TILE, 0)
+        spot = (pl.ds(pl.multiple_of(top, TILE), TILE), pl.ds(pl.multiple_of(left, TILE), TILE))
+        rows = pl.ds(pl.multiple_of(s % CAP * TILE, TILE), TILE)
+        acc_ref[spot] = acc_ref[spot] + arrived_ref[s // CAP, rows, :].astype(jnp.float32)
         return carry
 
-    lax.fori_loop(0, arrived_ref.shape[0], add, 0)
-    summed = acc_ref[...].astype(jnp.bfloat16)
+    lax.fori_loop(0, CAP * arrived_ref.shape[0], add, 0, unroll=4)
+    summed = acc_ref[0:rows_local, :].astype(jnp.bfloat16)
     out_ref[...] = summed
     panel_ref[...] = summed[2 * TILE :, 0:TILE]
 
@@ -339,7 +343,7 @@
         ),
         in_specs=[pl.BlockSpec(memory_space=pltpu.SMEM), vm, vm],
         out_specs=(vm, vm),
-        scratch_shapes=[pltpu.VMEM(front.shape, jnp.float32)],
+        scratch_shapes=[pltpu.VMEM((front.shape[0] + TILE, front.shape[1]), jnp.float32)],
         compiler_params=pltpu.CompilerParams(vmem_limit_bytes=48 * 1024 * 1024),
         cost_estimate=pl.CostEstimate(flops=10_000_000, bytes_accessed=30_000_000, transcendentals=0),
         name="extend_add",
@@ -373,20 +377,29 @@
         a_ref[step, rows_low:total, lanes] = col_ref[piece].reshape(cols_low, TILE)
 
     def solve_with(xh_ref, xl_ref):
-        def part(kk):
-            rows = pl.ds(pl.multiple_of(kk * width, width), width)
-            a = a_ref[kk]
+        def part(first, count):
+            rows = pl.ds(pl.multiple_of(first * width, width), count * width)
+            a = jnp.concatenate([a_ref[first + n] for n in range(count)], 1)
             return jnp.dot(a, xh_ref[rows, :], preferred_element_type=jnp.float32) + jnp.dot(
                 a, xl_ref[rows, :], preferred_element_type=jnp.float32
             )
 
-        def solve(kk, carry):
-            sum_ref[...] = sum_ref[...] + part(kk)
+        odd = (step + 1) % 2
+
+        @pl.when(odd == 1)
+        def _():
+            sum_ref[...] = part(0, 1)
+
+        @pl.when(odd == 0)
+        def _():
+            sum_ref[...] = jnp.zeros_like(sum_ref)
+
+        def solve(n, carry):
+            sum_ref[...] = sum_ref[...] + part(odd + 2 * n, 2)
             return carry
 
-        sum_ref[...] = jnp.zeros_like(sum_ref)
-        lax.fori_loop(0, step, solve, 0)
-        p_ref[...] = (sum_ref[...] + part(step)).astype(jnp.bfloat16)
+        lax.fori_loop(0, (step + 1) // 2, solve, 0)
+        p_ref[:, pl.ds(pl.multiple_of(step % 2 * width, width), width)] = sum_ref[...].astype(jnp.bfloat16)
 
     mid = xh1_ref.shape[0] // width
 
@@ -400,7 +413,7 @@
 
     @pl.when(step == c // 2)
     def _():
-        lane = pl.multiple_of(c % 2 * TILE, TILE)
+        lane = pl.multiple_of(c % 4 * TILE, TILE)
         rows = pl.ds(2 * TILE * cols_local, rows_low, stride=cols_local)
         out_ref[rows, :] = p_ref[0:rows_low, pl.ds(lane, TILE)].astype(jnp.float32)
 
@@ -410,7 +423,10 @@
         return carry
 
     chunk = rows_low
-    lax.fori_loop(0, 1, update, 0)
+
+    @pl.when(step % 2 == 1)
+    def _():
+        lax.fori_loop(0, 1, update, 0)
 
     @pl.when(step == steps - 1)
     def _():
@@ -451,7 +467,7 @@
         out_specs=vm,
         scratch_shapes=[
             pltpu.VMEM((steps, total, width), jnp.bfloat16),
-            pltpu.VMEM((total, width), jnp.bfloat16),
+            pltpu.VMEM((total, 2 * width), jnp.bfloat16),
             pltpu.VMEM((total, width), jnp.float32),
             pltpu.VMEM((tiles_row * TILE, tiles_col * TILE), jnp.float32),
         ],
@@ -480,17 +496,15 @@
     owner_hits = (owners[:, None] == jnp.arange(device_count)[None, :]).astype(jnp.int32)
     slot_rank = jnp.sum(jnp.cumsum(owner_hits, 0) * owner_hits, 1) - 1
     slot_index = owners * CAP + slot_rank
-
-    def exchange(x):
-        return lax.all_to_all(
-            x.reshape((device_count, CAP) + x.shape[1:]), both, split_axis=0, concat_axis=0, tiled=True
-        ).reshape(x.shape)
-
     targets = jnp.full((device_count * CAP,), -1, jnp.int32).at[slot_index].set(local_ids)
-    arrived = exchange(pack(slot_index, child_tiles))
-    flat_front = front.reshape(rows_local * TILE, cols_local * TILE)
-    targets, flat_front = lax.optimization_barrier((targets, flat_front))
-    assembled, panel = extend(exchange(targets), flat_front, arrived)
+    head = jnp.pad(
+        targets.astype(jnp.bfloat16).reshape(device_count, 1, CAP), ((0, 0), (0, HEAD - 1), (0, TILE - CAP))
+    )
+    arrived = lax.all_to_all(
+        pack(slot_index, child_tiles, head), both, split_axis=0, concat_axis=0, tiled=True
+    )
+    arrived_ids = arrived[:, CAP * TILE, 0:CAP].astype(jnp.int32).reshape(device_count * CAP)
+    assembled, panel = extend(arrived_ids, front.reshape(rows_local * TILE, cols_local * TILE), arrived)
     corner, panel = lax.optimization_barrier((corner, panel))
 
     place = jnp.stack([row_index, col_index]).astype(jnp.int32)

time: 353 us -> 340 us (0.963)
  starting transfers between devices: 40.3 us -> 23.9 us
  waiting for transfers between devices: 111 us -> 117 us
    all_gather x1, waiting for transfers between devices: 0.01 us -> 14.1 us  [per_device(): corner = lax.all_gather(corner, both, axis=0, tiled=False)]
    all_to_all x2 -> x1, waiting for transfers between devices: 111 us -> 102 us  [per_device(): lax.all_to_all(pack(slot_index, child_tiles, head), both, split_axis=0, c...]
    all_to_all x2 -> x1, starting transfers between devices: 19.1 us -> 11.9 us  [per_device(): lax.all_to_all(pack(slot_index, child_tiles, head), both, split_axis=0, c...]
    all_to_all x1, starting transfers between devices: 16.7 us -> 9.74 us  [per_device(): lax.all_to_all(pieces, 'row', split_axis=0, concat_axis=0, tiled=True)]
    unnamed x10 -> x8, local copies, waits for them, and re-layouts: 13.5 us -> 13.6 us
  transfers between devices with their start and end apart: 7 -> 6, of which waited for: 2 -> 2; matrix products, arithmetic and copies ran while one was open for 4% -> 5% of each run, Pallas kernels for 30% -> 32%
where the time goes in v4:
time: 340 us
  Pallas kernels  160 us (47%)
  waiting for transfers between devices  117 us (34%)
  starting transfers between devices  23.9 us (7%)
  local copies, waits for them, and re-layouts  18.9 us (6%)
  between operations  13.6 us (4%)
  other arithmetic  6.76 us (2%)
    all_to_all x1, waiting for transfers between devices, per_device(): lax.all_to_all(pack(slot_index, child_tiles, head), both, split_axis=0, c...  102 us
    pallas_call x2, Pallas kernels, factor_stage(): pl.pallas_call(functools.partial(factor_kernel, first, last), out_shape=t...  94.8 us
    pallas_call x1, Pallas kernels, finish(): pl.pallas_call(finish_kernel, grid=(steps,), out_shape=jax.ShapeDtypeStru...  51.9 us
    all_gather x1, waiting for transfers between devices, per_device(): corner = lax.all_gather(corner, both, axis=0, tiled=False)  14.1 us
    unnamed x8, local copies, waits for them, and re-layouts  13.6 us
    all_to_all x1, starting transfers between devices, per_device(): lax.all_to_all(pack(slot_index, child_tiles, head), both, split_axis=0, c...  11.9 us
    pallas_call x1, Pallas kernels, extend(): pl.pallas_call(extend_kernel, out_shape=(jax.ShapeDtypeStruct(front.shape...  10.9 us
    all_to_all x1, starting transfers between devices, per_device(): lax.all_to_all(pieces, 'row', split_axis=0, concat_axis=0, tiled=True)  9.74 us
  transfers between devices with their start and end apart: 6, of which 2 were waited for; matrix products, arithmetic and copies ran while one was open for 5% of the time, Pallas kernels for 32%

profile of v4, /device:TPU:1, one launch (start us, length us, event | category | flops | bytes accessed | tf_op | source)
XLA Modules:
  0.0 339.9 jit_solution(7540187316824936704)
XLA Ops:
  6.5 1.1 slice.20
  7.7 0.6 copy.22
  8.3 0.8 fusion.12
  9.1 0.1 fusion.2
  9.2 0.2 reduce_window_sum.11
  9.3 0.2 select_reduce_fusion
  9.5 0.8 fusion.9
  10.3 0.8 multiply_add_fusion
  11.1 1.0 scatter_custom_fusion
  12.1 0.2 reshape.43
  12.2 0.1 pad.4.head_ref
  12.3 2.2 copy-done.1
  14.5 2.5 pack_tiles.1
  17.0 3.4 %copy-done = bf16[128,272,128]{2,1,0:T(8,128)(2,1)} copy-done((bf16[128,272,128]{2,1,0:T(8,128)(2,1)}, bf16[128,272,128]{2,1,0:T(8,128)(2,1)S(1)}, u32[]{:S(2)}) %copy-start) | copy-done | bytes 8912920
  20.4 11.9 %all-to-all-start = ((bf16[128,272,128]{2,1,0:T(8,128)(2,1)}), bf16[128,272,128]{2,1,0:T(8,128)(2,1)}, u32[]{:S(2)}, u32[]{:S(2)}) async-start(bf16[128,272,128]{2,1,0:T(8,128)(2,1)} %copy-done), calls=%async_computation | async-start | bytes 17825792 | tf_op jit(solution)/shard_map/all_to_all | solution.py:503
  32.4 5.3 %copy.26 = bf16[256,8,8,128]{3,1,2,0:T(8,128)(2,1)} copy(bf16[256,8,8,128]{3,2,1,0:T(8,128)(2,1)} %bitcast.74) | data formatting | bytes 8388608
  37.7 102.5 %all-to-all-done.arrived_ref = bf16[128,272,128]{2,1,0:T(8,128)(2,1)} async-done(((bf16[128,272,128]{2,1,0:T(8,128)(2,1)}), bf16[128,272,128]{2,1,0:T(8,128)(2,1)}, u32[]{:S(2)}, u32[]{:S(2)}) %all-to-all-start) | async-done | bytes 8912928 | tf_op jit(solution)/shard_map/all_to_all | solution.py:503
  140.2 1.2 fusion.1
  141.3 0.1 reshape.33.id_ref
  141.5 10.9 %extend_add.1 = (bf16[2048,1024]{1,0:T(8,128)(2,1)S(1)}, bf16[1792,128]{1,0:T(8,128)(2,1)}) custom-call(s32[256]{0:T(256)S(1)} %reshape.33.id_ref, bf16[2048,1024]{1,0:T(8,128)(2,1)} %bitcast.73, bf16[128,272,128]{2,1,0:T(8,128)(2,1)} %all-to-all-done.arrived_ref), custom_call_target="tpu_custom_call" | custom-call | flops 10000000 | bytes 30000000 | tf_op jit(solution)/shard_map/extend_add/pallas_call | solution.py:338
  152.4 2.1 copy-done.2
  154.4 14.1 %all-gather.6.cloned.1.call-done = bf16[256,1,128,1,1,128]{5,2,4,3,1,0:T(8,128)(2,1)} async-done(((bf16[2,1,128,1,1,128]{5,2,4,3,1,0:T(8,128)(2,1)}), bf16[256,1,128,1,1,128]{5,2,4,3,1,0:T(8,128)(2,1)}) %all-gather.6.cloned.1.call-update) | async-done | bytes 8388624 | tf_op jit(solution)/shard_map/all_gather | solution.py:492
  168.6 0.6 pad_add_fusion.place_ref
  169.2 1.1 fusion
  170.3 2.0 collective-permute-start
  172.3 1.1 select_bitcast_fusion.2
  173.4 0.3 collective-permute-start.1
  173.6 29.1 %factor_corner.2 = (bf16[2,128,128]{2,1,0:T(8,128)(2,1)}, bf16[512,512]{1,0:T(8,128)(2,1)}, bf16[512,512]{1,0:T(8,128)(2,1)}, f32[6,2048,256]{2,1,0:T(8,128)}, b...) custom-call(s32[2]{0:T(128)} %pad_add_fusion.place_ref, s32[256]{0:T(256)} %constant.102.clone.unit_ref, ...), custom_call_target="tpu_custom_call" | custom-call | flops 60000002048 | bytes 24000000 | tf_op jit(solution)/shard_map/factor_corner/pallas_call | solution.py:268
  202.8 2.7 broadcast_in_dim.10
  205.6 9.7 %all-to-all-start.1 = ((bf16[8,2,7,128,128]{4,3,2,1,0:T(8,128)(2,1)}), bf16[8,2,7,128,128]{4,3,2,1,0:T(8,128)(2,1)}, u32[]{:S(2)}, u32[]{:S(2)}) async-start(bf16[8,2,7,128,128]{4,3,2,1,0:T(8,128)(2,1)} %broadcast_in_dim.10), calls=%async_computation.1 | async-start | bytes 7340032 | tf_op jit(solution)/shard_map/all_to_all | solution.py:532
  215.3 65.7 %factor_corner.3 = (bf16[2,128,128]{2,1,0:T(8,128)(2,1)}, bf16[2048,1536]{1,0:T(8,128)(2,1)}, bf16[2048,1536]{1,0:T(8,128)(2,1)}) custom-call(s32[2]{0:T(128)} %pad_add_fusion.place_ref, s32[256]{0:T(256)} %constant.103.clone.unit_ref, f32[6,2048,256]{2,1,0:T(8,128)} %get-tuple-element.30.rest_0_, bf16[2048,256]{1,0:T(8,128)(2,1)} %get-tuple-element.31.rest_1_, ...), custom_call_target="tpu_custom_call" | custom-call | flops 60000002048 | bytes 24000000 | tf_op jit(solution)/shard_map/factor_corner/pallas_call | solution.py:268
  281.1 51.9 %solve_update.1 = f32[16384,128]{1,0:T(8,128)} custom-call(s32[2]{0:T(128)} %pad_add_fusion.place_ref, bf16[512,512]{1,0:T(8,128)(2,1)} %get-tuple-element.24.xh1_ref, bf16[512,512]{1,0:T(8,128)(2,1)} %get-tuple-element.25.xl1_ref, bf16[2048,1536]{1,0:T(8,128)(2,1)} %get-tuple-element.33.xh2_ref, bf16[2048,1536]{1,0:T(8,128)(2,1)} %get-tuple-element.34.xl2_ref, ...), custom_call_target="tpu_custom_call" | custom-call | flops 40000000000 | bytes 50000000 | tf_op jit(solution)/shard_map/solve_update/pallas_call | solution.py:451
  (14 shorter events, 0.2 us)
Async XLA Ops:
  6.5 162.0 %all-gather.6.cloned.1.call-start = ((), (), s32[]{:S(2)}) async-start(), calls=%async_computation.3 | async-start | bytes 8454144 | tf_op jit(solution)/shard_map/all_gather | solution.py:492
  12.3 2.2 copy-start.1
  17.0 3.4 %copy-start = (bf16[128,272,128]{2,1,0:T(8,128)(2,1)}, bf16[128,272,128]{2,1,0:T(8,128)(2,1)S(1)}, u32[]{:S(2)}) copy-start(bf16[128,272,128]{2,1,0:T(8,128)(2,1)S(1)} %pack_tiles.1) | copy-start | bytes 26738692
  20.4 119.7 %all-to-all-start = ((bf16[128,272,128]{2,1,0:T(8,128)(2,1)}), bf16[128,272,128]{2,1,0:T(8,128)(2,1)}, u32[]{:S(2)}, u32[]{:S(2)}) async-start(bf16[128,272,128]{2,1,0:T(8,128)(2,1)} %copy-done), calls=%async_computation | async-start | bytes 17825792 | tf_op jit(solution)/shard_map/all_to_all | solution.py:503
  32.3 248.7 %all-gather.4.cloned.1.call-start = ((), (), s32[]{:S(2)}) async-start(), calls=%async_computation.2 | async-start | bytes 7798784 | tf_op jit(solution)/shard_map/all_gather | solution.py:514
  152.4 2.1 copy-start.2
  170.3 32.4 %collective-permute-start = (bf16[7,128,128]{2,1,0:T(8,128)(2,1)S(1)}, bf16[7,128,128]{2,1,0:T(8,128)(2,1)S(1)}, u32[]{:S(2)}, u32[]{:S(2)}) collective-permute-start(bf16[7,128,128]{2,1,0:T(8,128)(2,1)S(1)} %fusion), channel_id=1, source_target_pairs={{0,0},{1,8},{2,16},{3,24},{4,32},{5,40},{6,48},{7,56},{8,64},{9,72... | collective-permute-start | bytes 688136 | tf_op jit(solution)/shard_map/ppermute | solution.py:526
  173.4 29.4 %collective-permute-start.1 = (bf16[7,128,128]{2,1,0:T(8,128)(2,1)S(1)}, bf16[7,128,128]{2,1,0:T(8,128)(2,1)S(1)}, u32[]{:S(2)}, u32[]{:S(2)}) collective-permute-start(bf16[7,128,128]{2,1,0:T(8,128)(2,1)S(1)} %select_bitcast_fusion.2), channel_id=1, source_target_pairs={{0,8},{1,0},{2,24},{3,16},{4,40},{5,32},{6,56},{7,48},{8,72},{9,64... | collective-permute-start | bytes 688136 | tf_op jit(solution)/shard_map/ppermute | solution.py:526
  205.6 75.5 %all-to-all-start.1 = ((bf16[8,2,7,128,128]{4,3,2,1,0:T(8,128)(2,1)}), bf16[8,2,7,128,128]{4,3,2,1,0:T(8,128)(2,1)}, u32[]{:S(2)}, u32[]{:S(2)}) async-start(bf16[8,2,7,128,128]{4,3,2,1,0:T(8,128)(2,1)} %broadcast_in_dim.10), calls=%async_computation.1 | async-start | bytes 7340032 | tf_op jit(solution)/shard_map/all_to_all | solution.py:532
Sparse Core Ops, SparseCore 0:
  10.3 158.1 all-gather.5
  170.2 75.7 all-gather.3

commit v5 on v4

--- a/solution.py
+++ b/solution.py
@@ -9,7 +9,6 @@
 
 CAP = 2
 HEAD = 16
-SPLIT = 2
 PANEL = 2048
 TILE = 128
 NT_DIMS = (((1,), (1,)), ((), ()))
@@ -104,35 +103,15 @@
 def factor_kernel(first, last, place_ref, unit_ref, *rest):
     tiles = PANEL // TILE
     pairs = tiles // 2
-    if first == 0:
-        source_ref, rest = rest[0], rest[1:]
-    else:
-        source_ref, oldh_ref, oldl_ref = rest[:3]
-        rest = rest[3:]
-    own_ref, xh_ref, xl_ref = rest[:3]
-    rest = rest[3:]
-    if last < pairs:
-        next_ref, nexth_ref, nextl_ref = rest[:3]
-        rest = rest[3:]
+    source_ref, own_ref, xh_ref, xl_ref, *rest = rest
     m_ref, eh_ref, el_ref, a_ref, o_ref, i_ref, s_ref, t_ref, sem = rest
-    if first == 0:
-        for j in range(tiles):
-            for i in range(tiles):
-                spot = (j // 2, slice(i * TILE, (i + 1) * TILE), slice(j % 2 * TILE, (j % 2 + 1) * TILE))
-                if i >= j:
-                    m_ref[spot] = source_ref[i % 8 * 16 + j, i // 8].astype(jnp.float32)
-                else:
-                    m_ref[spot] = jnp.zeros((TILE, TILE), jnp.float32)
-    else:
-        loads = (
-            pltpu.make_async_copy(source_ref, m_ref.at[pl.ds(0, pairs - first)], sem.at[0]),
-            pltpu.make_async_copy(oldh_ref, eh_ref.at[(first - 1) % 2], sem.at[1]),
-            pltpu.make_async_copy(oldl_ref, el_ref.at[(first - 1) % 2], sem.at[2]),
-        )
-        for load in loads:
-            load.start()
-        for load in loads:
-            load.wait()
+    for j in range(tiles):
+        for i in range(tiles):
+            spot = (j // 2, slice(i * TILE, (i + 1) * TILE), slice(j % 2 * TILE, (j % 2 + 1) * TILE))
+            if i >= j:
+                m_ref[spot] = source_ref[i % 8 * 16 + j, i // 8].astype(jnp.float32)
+            else:
+                m_ref[spot] = jnp.zeros((TILE, TILE), jnp.float32)
     own_ref[...] = jnp.zeros_like(own_ref)
     r = place_ref[0]
     c = place_ref[1]
@@ -186,6 +165,13 @@
             eh_ref[buf, rows, lanes] = eh
             el_ref[buf, rows, lanes] = el
 
+    def keep_inverse(p, buf):
+        wide = pl.ds(pl.multiple_of(p * 256, 256), 256)
+        return (
+            pltpu.make_async_copy(eh_ref.at[buf], xh_ref.at[:, wide], sem.at[0, buf]),
+            pltpu.make_async_copy(el_ref.at[buf], xl_ref.at[:, wide], sem.at[1, buf]),
+        )
+
     def step(p, carry):
         local = p - first
         buf = p % 2
@@ -210,6 +196,11 @@
         invert_tile(a_ref, i_ref, s_ref, t_ref, first_beside)
         m_ref[local, tile_rows(k), 0:TILE] = identity
         m_ref[local, tile_rows(k), TILE:] = jnp.zeros((TILE, TILE), jnp.float32)
+        @pl.when(p >= 2)
+        def _():
+            for copy in keep_inverse(p - 2, buf):
+                copy.wait()
+
         column(p, buf, 0)
         keep_own(k, buf, 0)
 
@@ -238,40 +229,33 @@
         keep_own(k + 1, buf, 1)
         eh_ref[buf, tile_rows(k + 1), 0:TILE] = zero
         el_ref[buf, tile_rows(k + 1), 0:TILE] = zero
-        wide = pl.ds(pl.multiple_of(local * 256, 256), 256)
-        depth = last * 256
-        xh_ref[:, wide] = eh_ref[buf, 0:depth, :]
-        xl_ref[:, wide] = el_ref[buf, 0:depth, :]
+        for copy in keep_inverse(p, buf):
+            copy.start()
         return carry
 
     lax.fori_loop(first, last, step, 0)
-    if last < pairs:
-        next_ref[...] = m_ref[last - first : pairs - first]
-        nexth_ref[...] = eh_ref[(last - 1) % 2]
-        nextl_ref[...] = el_ref[(last - 1) % 2]
-
-
-def factor_stage(first, last, place, *sources):
+    for p in (pairs - 2, pairs - 1):
+        for copy in keep_inverse(p, p % 2):
+            copy.wait()
+
+
+def factor_corner(place, corner):
     pairs = PANEL // 256
     vm = pl.BlockSpec(memory_space=pltpu.VMEM)
+    hbm = pl.BlockSpec(memory_space=pl.ANY)
     smem = pl.BlockSpec(memory_space=pltpu.SMEM)
-    wide = (last - first) * 256
-    out_shape = [
-        jax.ShapeDtypeStruct((2, TILE, TILE), jnp.bfloat16),
-        jax.ShapeDtypeStruct((last * 256, wide), jnp.bfloat16),
-        jax.ShapeDtypeStruct((last * 256, wide), jnp.bfloat16),
-    ]
-    if last < pairs:
-        out_shape.append(jax.ShapeDtypeStruct((pairs - last, PANEL, 256), jnp.float32))
-        out_shape += [jax.ShapeDtypeStruct((PANEL, 256), jnp.bfloat16)] * 2
     tile = pltpu.VMEM((TILE, TILE), jnp.float32)
     return pl.pallas_call(
-        functools.partial(factor_kernel, first, last),
-        out_shape=tuple(out_shape),
-        in_specs=[smem, smem] + ([vm] if first == 0 else [pl.BlockSpec(memory_space=pl.ANY)] * 3),
-        out_specs=tuple(vm for _ in out_shape),
+        functools.partial(factor_kernel, 0, pairs),
+        out_shape=(
+            jax.ShapeDtypeStruct((2, TILE, TILE), jnp.bfloat16),
+            jax.ShapeDtypeStruct((PANEL, PANEL), jnp.bfloat16),
+            jax.ShapeDtypeStruct((PANEL, PANEL), jnp.bfloat16),
+        ),
+        in_specs=[smem, smem, vm],
+        out_specs=(vm, hbm, hbm),
         scratch_shapes=[
-            pltpu.VMEM((pairs - first + 1, PANEL, 256), jnp.float32),
+            pltpu.VMEM((pairs + 1, PANEL, 256), jnp.float32),
             pltpu.VMEM((2, PANEL, 256), jnp.bfloat16),
             pltpu.VMEM((2, PANEL, 256), jnp.bfloat16),
             tile,
@@ -279,12 +263,12 @@
             tile,
             tile,
             tile,
-            pltpu.SemaphoreType.DMA((3,)),
+            pltpu.SemaphoreType.DMA((2, 2)),
         ],
-        compiler_params=pltpu.CompilerParams(vmem_limit_bytes=60 * 1024 * 1024),
-        cost_estimate=pl.CostEstimate(flops=60_000_000_000, bytes_accessed=24_000_000, transcendentals=0),
+        compiler_params=pltpu.CompilerParams(vmem_limit_bytes=56 * 1024 * 1024),
+        cost_estimate=pl.CostEstimate(flops=90_000_000_000, bytes_accessed=24_000_000, transcendentals=0),
         name="factor_corner",
-    )(place, jnp.asarray(unit_table(first, last)), *sources)
+    )(place, jnp.asarray(unit_table(0, pairs)), corner)
 
 
 def pack_kernel(slot_ref, child_ref, head_ref, packed_ref):
@@ -351,7 +335,7 @@
 
 
 def finish_kernel(
-    place_ref, xh1_ref, xl1_ref, xh2_ref, xl2_ref, row_ref, col_ref, own1_ref, own2_ref, assembled_ref, out_ref, a_ref, p_ref, sum_ref, acc_ref
+    place_ref, xh_ref, xl_ref, row_ref, col_ref, own_ref, assembled_ref, out_ref, a_ref, p_ref, sum_ref, acc_ref
 ):
     step = pl.program_id(0)
     steps = PANEL // (2 * TILE)
@@ -368,7 +352,7 @@
         out_ref[0:top, :] = jnp.zeros((top, TILE), jnp.float32)
         for a in range(2):
             rows = pl.ds(a * TILE * cols_local, TILE, stride=cols_local)
-            out_ref[rows, :] = own1_ref[a].astype(jnp.float32) + own2_ref[a].astype(jnp.float32)
+            out_ref[rows, :] = own_ref[a].astype(jnp.float32)
         acc_ref[...] = assembled_ref[2 * TILE :, TILE:].astype(jnp.float32)
 
     for piece in range(2):
@@ -376,40 +360,29 @@
         a_ref[step, 0:rows_low, lanes] = row_ref[piece].reshape(rows_low, TILE)
         a_ref[step, rows_low:total, lanes] = col_ref[piece].reshape(cols_low, TILE)
 
-    def solve_with(xh_ref, xl_ref):
-        def part(first, count):
-            rows = pl.ds(pl.multiple_of(first * width, width), count * width)
-            a = jnp.concatenate([a_ref[first + n] for n in range(count)], 1)
-            return jnp.dot(a, xh_ref[rows, :], preferred_element_type=jnp.float32) + jnp.dot(
-                a, xl_ref[rows, :], preferred_element_type=jnp.float32
-            )
-
-        odd = (step + 1) % 2
-
-        @pl.when(odd == 1)
-        def _():
-            sum_ref[...] = part(0, 1)
-
-        @pl.when(odd == 0)
-        def _():
-            sum_ref[...] = jnp.zeros_like(sum_ref)
-
-        def solve(n, carry):
-            sum_ref[...] = sum_ref[...] + part(odd + 2 * n, 2)
-            return carry
-
-        lax.fori_loop(0, (step + 1) // 2, solve, 0)
-        p_ref[:, pl.ds(pl.multiple_of(step % 2 * width, width), width)] = sum_ref[...].astype(jnp.bfloat16)
-
-    mid = xh1_ref.shape[0] // width
-
-    @pl.when(step < mid)
+    def part(first, count):
+        rows = pl.ds(pl.multiple_of(first * width, width), count * width)
+        a = jnp.concatenate([a_ref[first + n] for n in range(count)], 1)
+        return jnp.dot(a, xh_ref[rows, :], preferred_element_type=jnp.float32) + jnp.dot(
+            a, xl_ref[rows, :], preferred_element_type=jnp.float32
+        )
+
+    odd = (step + 1) % 2
+
+    @pl.when(odd == 1)
     def _():
-        solve_with(xh1_ref, xl1_ref)
-
-    @pl.when(step >= mid)
+        sum_ref[...] = part(0, 1)
+
+    @pl.when(odd == 0)
     def _():
-        solve_with(xh2_ref, xl2_ref)
+        sum_ref[...] = jnp.zeros_like(sum_ref)
+
+    def solve(n, carry):
+        sum_ref[...] = sum_ref[...] + part(odd + 2 * n, 2)
+        return carry
+
+    lax.fori_loop(0, (step + 1) // 2, solve, 0)
+    p_ref[:, pl.ds(pl.multiple_of(step % 2 * width, width), width)] = sum_ref[...].astype(jnp.bfloat16)
 
     @pl.when(step == c // 2)
     def _():
@@ -438,29 +411,24 @@
         lax.fori_loop(1, cols_local, write, 0)
 
 
-def finish(place, x1, x2, row_raw, col_raw, own1, own2, assembled):
+def finish(place, xh, xl, row_raw, col_raw, own, assembled):
     width = 2 * TILE
     steps = PANEL // width
-    mid = x1[0].shape[1] // width
     tiles_row = row_raw.shape[1]
     tiles_col = col_raw.shape[1]
     total = (tiles_row + tiles_col) * TILE
     vm = pl.BlockSpec(memory_space=pltpu.VMEM)
-    early = pl.BlockSpec((mid * width, width), lambda s: (0, jnp.minimum(s, mid - 1)))
-    late = pl.BlockSpec((PANEL, width), lambda s: (0, jnp.maximum(s - mid, 0)))
+    inverse = pl.BlockSpec((PANEL, width), lambda s: (0, s))
     return pl.pallas_call(
         finish_kernel,
         grid=(steps,),
         out_shape=jax.ShapeDtypeStruct((assembled.shape[0] * assembled.shape[1] // TILE, TILE), jnp.float32),
         in_specs=[
             pl.BlockSpec(memory_space=pltpu.SMEM),
-            early,
-            early,
-            late,
-            late,
+            inverse,
+            inverse,
             pl.BlockSpec((2, tiles_row, TILE, TILE), lambda s: (s, 0, 0, 0)),
             pl.BlockSpec((2, tiles_col, TILE, TILE), lambda s: (s, 0, 0, 0)),
-            vm,
             vm,
             vm,
         ],
@@ -476,7 +444,7 @@
         ),
         cost_estimate=pl.CostEstimate(flops=40_000_000_000, bytes_accessed=50_000_000, transcendentals=0),
         name="solve_update",
-    )(place, *x1, *x2, row_raw, col_raw, own1, own2, assembled)
+    )(place, xh, xl, row_raw, col_raw, own, assembled)
 
 
 def per_device(front, child_tiles, tile_map):
@@ -505,10 +473,6 @@
     )
     arrived_ids = arrived[:, CAP * TILE, 0:CAP].astype(jnp.int32).reshape(device_count * CAP)
     assembled, panel = extend(arrived_ids, front.reshape(rows_local * TILE, cols_local * TILE), arrived)
-    corner, panel = lax.optimization_barrier((corner, panel))
-
-    place = jnp.stack([row_index, col_index]).astype(jnp.int32)
-    own1, xh1, xl1, *state = factor_stage(0, SPLIT, place, corner)
     low_tiles = rows_local - 2
     panel = panel.reshape(low_tiles, TILE, TILE)
     row_raw = lax.all_gather(panel, "col", axis=0, tiled=False)
@@ -528,12 +492,13 @@
     first = jnp.where(high == 0, received[0], received[1])
     second = jnp.where(high == 0, received[1], received[0])
     pieces = jnp.broadcast_to(jnp.stack([first, second]), (row_count, 2) + first.shape)
-    *state, pieces = lax.optimization_barrier((*state, pieces))
+    corner, pieces = lax.optimization_barrier((corner, pieces))
     col_raw = lax.all_to_all(
         pieces, "row", split_axis=0, concat_axis=0, tiled=True
     ).reshape(col_count, low_tiles // 2, TILE, TILE)
-    own2, xh2, xl2 = factor_stage(SPLIT, PANEL // 256, place, *state)
-    out = finish(place, (xh1, xl1), (xh2, xl2), row_raw, col_raw, own1, own2, assembled)
+    place = jnp.stack([row_index, col_index]).astype(jnp.int32)
+    own, xh, xl = factor_corner(place, corner)
+    out = finish(place, xh, xl, row_raw, col_raw, own, assembled)
     return out.reshape(rows_local, 1, TILE, cols_local, 1, TILE)
 
 

time: 340 us -> 332 us (0.976)
  Pallas kernels: 160 us -> 144 us
  waiting for transfers between devices: 117 us -> 128 us
  starting transfers between devices: 23.9 us -> 19.3 us
    ppermute x2, waiting for transfers between devices: 0.01 us -> 23 us  [per_device(): received.append(lax.ppermute(outgoing, both, pairs))]
    pallas_call x2 -> x1, Pallas kernels: 94.8 us -> 79.5 us  [factor_corner(): pl.pallas_call(functools.partial(factor_kernel, 0, pairs), out_shape=(jax...]
    all_gather x1, waiting for transfers between devices: 14.1 us -> 3.07 us  [per_device(): corner = lax.all_gather(corner, both, axis=0, tiled=False)]
    all_to_all x1, starting transfers between devices: 9.74 us -> 4.69 us  [per_device(): lax.all_to_all(pieces, 'row', split_axis=0, concat_axis=0, tiled=True)]
  transfers between devices with their start and end apart: 6 -> 6, of which waited for: 2 -> 4; matrix products, arithmetic and copies ran while one was open for 5% -> 5% of each run, Pallas kernels for 32% -> 28%
where the time goes in v5:
time: 332 us; the launch traced here: 331 us
  Pallas kernels  144 us (43%)
  waiting for transfers between devices  128 us (39%)
  starting transfers between devices  19.3 us (6%)
  local copies, waits for them, and re-layouts  18.7 us (6%)
  between operations  13.6 us (4%)
  other arithmetic  7.01 us (2%)
    all_to_all x1, waiting for transfers between devices, per_device(): lax.all_to_all(pack(slot_index, child_tiles, head), both, split_axis=0, c...  102 us
    pallas_call x1, Pallas kernels, factor_corner(): pl.pallas_call(functools.partial(factor_kernel, 0, pairs), out_shape=(jax...  79.5 us
    pallas_call x1, Pallas kernels, finish(): pl.pallas_call(finish_kernel, grid=(steps,), out_shape=jax.ShapeDtypeStru...  51.4 us
    ppermute x2, waiting for transfers between devices, per_device(): received.append(lax.ppermute(outgoing, both, pairs))  23 us
    unnamed x8, local copies, waits for them, and re-layouts  13.5 us
    all_to_all x1, starting transfers between devices, per_device(): lax.all_to_all(pack(slot_index, child_tiles, head), both, split_axis=0, c...  11.9 us
    pallas_call x1, Pallas kernels, extend(): pl.pallas_call(extend_kernel, out_shape=(jax.ShapeDtypeStruct(front.shape...  11 us
  transfers between devices with their start and end apart: 6, of which 4 were waited for; matrix products, arithmetic and copies ran while one was open for 5% of the time, Pallas kernels for 28%

profile of v5, /device:TPU:1, one launch (start us, length us, event | category | flops | bytes accessed | tf_op | source)
XLA Modules:
  0.0 331.4 jit_solution(2330300643560852464)
XLA Ops:
  6.5 1.1 slice.20
  7.7 0.6 copy.21
  8.3 0.8 fusion.12
  9.2 0.2 reduce_window_sum.11
  9.3 0.2 select_reduce_fusion
  9.5 0.8 fusion.9
  10.3 0.8 multiply_add_fusion
  11.1 1.0 scatter_custom_fusion
  12.1 0.2 reshape.43
  12.2 0.1 pad.4.head_ref
  12.4 2.2 copy-done.1
  14.5 2.5 pack_tiles.1
  17.0 3.4 %copy-done = bf16[128,272,128]{2,1,0:T(8,128)(2,1)} copy-done((bf16[128,272,128]{2,1,0:T(8,128)(2,1)}, bf16[128,272,128]{2,1,0:T(8,128)(2,1)S(1)}, u32[]{:S(2)}) %copy-start) | copy-done | bytes 8912920
  20.4 11.9 %all-to-all-start = ((bf16[128,272,128]{2,1,0:T(8,128)(2,1)}), bf16[128,272,128]{2,1,0:T(8,128)(2,1)}, u32[]{:S(2)}, u32[]{:S(2)}) async-start(bf16[128,272,128]{2,1,0:T(8,128)(2,1)} %copy-done), calls=%async_computation | async-start | bytes 17825792 | tf_op jit(solution)/shard_map/all_to_all | solution.py:471
  32.4 5.3 %copy.25 = bf16[256,8,8,128]{3,1,2,0:T(8,128)(2,1)} copy(bf16[256,8,8,128]{3,2,1,0:T(8,128)(2,1)} %bitcast.74) | data formatting | bytes 8388608
  37.7 102.4 %all-to-all-done.arrived_ref = bf16[128,272,128]{2,1,0:T(8,128)(2,1)} async-done(((bf16[128,272,128]{2,1,0:T(8,128)(2,1)}), bf16[128,272,128]{2,1,0:T(8,128)(2,1)}, u32[]{:S(2)}, u32[]{:S(2)}) %all-to-all-start) | async-done | bytes 8912928 | tf_op jit(solution)/shard_map/all_to_all | solution.py:471
  140.1 1.2 fusion.1
  141.2 0.1 reshape.33.id_ref
  141.4 11.0 %extend_add.1 = (bf16[2048,1024]{1,0:T(8,128)(2,1)S(1)}, bf16[1792,128]{1,0:T(8,128)(2,1)}) custom-call(s32[256]{0:T(256)S(1)} %reshape.33.id_ref, bf16[2048,1024]{1,0:T(8,128)(2,1)} %bitcast.73, bf16[128,272,128]{2,1,0:T(8,128)(2,1)} %all-to-all-done.arrived_ref), custom_call_target="tpu_custom_call" | custom-call | flops 10000000 | bytes 30000000 | tf_op jit(solution)/shard_map/extend_add/pallas_call | solution.py:322
  152.4 1.9 copy-done.2
  154.3 1.2 select_bitcast_fusion.2
  155.5 0.7 collective-permute-start.1
  156.2 1.2 fusion
  157.4 1.9 collective-permute-start
  159.4 0.6 pad_add_fusion.place_ref
  160.0 20.8 %collective-permute-done.1 = bf16[7,128,128]{2,1,0:T(8,128)(2,1)S(1)} collective-permute-done((bf16[7,128,128]{2,1,0:T(8,128)(2,1)S(1)}, bf16[7,128,128]{2,1,0:T(8,128)(2,1)S(1)}, u32[]{:S(2)}, u32[]{:S(2)}) %collective-permute-start.1) | collective-permute-done | bytes 229408 | tf_op jit(solution)/shard_map/ppermute | solution.py:490
  180.9 2.2 collective-permute-done
  183.1 3.1 all-gather.6.cloned.1.call-done
  186.2 2.7 broadcast_in_dim.10
  188.9 4.7 %all-to-all-start.1 = ((bf16[8,2,7,128,128]{4,3,2,1,0:T(8,128)(2,1)}), bf16[8,2,7,128,128]{4,3,2,1,0:T(8,128)(2,1)}, u32[]{:S(2)}, u32[]{:S(2)}) async-start(bf16[8,2,7,128,128]{4,3,2,1,0:T(8,128)(2,1)} %broadcast_in_dim.10), calls=%async_computation.1 | async-start | bytes 7340032 | tf_op jit(solution)/shard_map/all_to_all | solution.py:496
  193.6 79.5 %factor_corner.1 = (bf16[2,128,128]{2,1,0:T(8,128)(2,1)}, bf16[2048,2048]{1,0:T(8,128)(2,1)}, bf16[2048,2048]{1,0:T(8,128)(2,1)}) custom-call(s32[2]{0:T(128)} %pad_add_fusion.place_ref, s32[256]{0:T(256)} %constant.100.clone.unit_ref, bf16[128,2,128,128]{3,2,1,0:T(8,128)(2,1)} %bitcast.75), custom_call_target="tpu_custom_call" | custom-call | flops 89999998976 | bytes 24000000 | tf_op jit(solution)/shard_map/factor_corner/pallas_call | solution.py:248
  273.2 51.4 %solve_update.1 = f32[16384,128]{1,0:T(8,128)} custom-call(s32[2]{0:T(128)} %pad_add_fusion.place_ref, bf16[2048,2048]{1,0:T(8,128)(2,1)} %get-tuple-element.14.xh_ref, bf16[2048,2048]{1,0:T(8,128)(2,1)} %get-tuple-element.15.xl_ref, bf16[16,14,128,128]{3,2,1,0:T(8,128)(2,1)} %all-gather.4.cloned.1.call-done.row_ref, ...), custom_call_target="tpu_custom_call" | custom-call | flops 40000000000 | bytes 50000000 | tf_op jit(solution)/shard_map/solve_update/pallas_call | solution.py:422
  (13 shorter events, 0.3 us)
Async XLA Ops:
  6.5 179.7 %all-gather.6.cloned.1.call-start = ((), (), s32[]{:S(2)}) async-start(), calls=%async_computation.3 | async-start | bytes 8454144 | tf_op jit(solution)/shard_map/all_gather | solution.py:460
  12.3 2.2 copy-start.1
  17.0 3.4 %copy-start = (bf16[128,272,128]{2,1,0:T(8,128)(2,1)}, bf16[128,272,128]{2,1,0:T(8,128)(2,1)S(1)}, u32[]{:S(2)}) copy-start(bf16[128,272,128]{2,1,0:T(8,128)(2,1)S(1)} %pack_tiles.1) | copy-start | bytes 26738692
  20.4 119.6 %all-to-all-start = ((bf16[128,272,128]{2,1,0:T(8,128)(2,1)}), bf16[128,272,128]{2,1,0:T(8,128)(2,1)}, u32[]{:S(2)}, u32[]{:S(2)}) async-start(bf16[128,272,128]{2,1,0:T(8,128)(2,1)} %copy-done), calls=%async_computation | async-start | bytes 17825792 | tf_op jit(solution)/shard_map/all_to_all | solution.py:471
  32.3 240.9 %all-gather.4.cloned.1.call-start = ((), (), s32[]{:S(2)}) async-start(), calls=%async_computation.2 | async-start | bytes 7798784 | tf_op jit(solution)/shard_map/all_gather | solution.py:478
  152.4 1.9 copy-start.2
  155.5 25.3 %collective-permute-start.1 = (bf16[7,128,128]{2,1,0:T(8,128)(2,1)S(1)}, bf16[7,128,128]{2,1,0:T(8,128)(2,1)S(1)}, u32[]{:S(2)}, u32[]{:S(2)}) collective-permute-start(bf16[7,128,128]{2,1,0:T(8,128)(2,1)S(1)} %select_bitcast_fusion.2), channel_id=1, source_target_pairs={{0,8},{1,0},{2,24},{3,16},{4,40},{5,32},{6,56},{7,48},{8,72},{9,64... | collective-permute-start | bytes 688136 | tf_op jit(solution)/shard_map/ppermute | solution.py:490
  157.4 25.6 %collective-permute-start = (bf16[7,128,128]{2,1,0:T(8,128)(2,1)S(1)}, bf16[7,128,128]{2,1,0:T(8,128)(2,1)S(1)}, u32[]{:S(2)}, u32[]{:S(2)}) collective-permute-start(bf16[7,128,128]{2,1,0:T(8,128)(2,1)S(1)} %fusion), channel_id=1, source_target_pairs={{0,0},{1,8},{2,16},{3,24},{4,32},{5,40},{6,48},{7,56},{8,64},{9,72... | collective-permute-start | bytes 688136 | tf_op jit(solution)/shard_map/ppermute | solution.py:490
  188.9 84.2 %all-to-all-start.1 = ((bf16[8,2,7,128,128]{4,3,2,1,0:T(8,128)(2,1)}), bf16[8,2,7,128,128]{4,3,2,1,0:T(8,128)(2,1)}, u32[]{:S(2)}, u32[]{:S(2)}) async-start(bf16[8,2,7,128,128]{4,3,2,1,0:T(8,128)(2,1)} %broadcast_in_dim.10), calls=%async_computation.1 | async-start | bytes 7340032 | tf_op jit(solution)/shard_map/all_to_all | solution.py:496
Sparse Core Ops, SparseCore 0:
  10.3 175.8 all-gather.5
  187.9 80.2 all-gather.3

commit v6 on v5

--- a/solution.py
+++ b/solution.py
@@ -468,11 +468,11 @@
     head = jnp.pad(
         targets.astype(jnp.bfloat16).reshape(device_count, 1, CAP), ((0, 0), (0, HEAD - 1), (0, TILE - CAP))
     )
-    arrived = lax.all_to_all(
-        pack(slot_index, child_tiles, head), both, split_axis=0, concat_axis=0, tiled=True
-    )
+    flat_front = front.reshape(rows_local * TILE, cols_local * TILE)
+    packed, flat_front = lax.optimization_barrier((pack(slot_index, child_tiles, head), flat_front))
+    arrived = lax.all_to_all(packed, both, split_axis=0, concat_axis=0, tiled=True)
     arrived_ids = arrived[:, CAP * TILE, 0:CAP].astype(jnp.int32).reshape(device_count * CAP)
-    assembled, panel = extend(arrived_ids, front.reshape(rows_local * TILE, cols_local * TILE), arrived)
+    assembled, panel = extend(arrived_ids, flat_front, arrived)
     low_tiles = rows_local - 2
     panel = panel.reshape(low_tiles, TILE, TILE)
     row_raw = lax.all_gather(panel, "col", axis=0, tiled=False)

time: 332 us -> 336 us (1.012); the launches traced: 331 us -> 331 us
  blocking collectives: 0 us -> 118 us
  waiting for transfers between devices: 128 us -> 23.7 us
  starting transfers between devices: 19.3 us -> 7.98 us
    all_to_all x0 -> x1, blocking collectives: none -> 118 us  [per_device(): lax.all_to_all(packed, both, split_axis=0, concat_axis=0, tiled=True)]
    all_to_all x1 -> x0, waiting for transfers between devices: 102 us -> none  [per_device(): lax.all_to_all(pack(slot_index, child_tiles, head), both, split_axis=0, c...]
    all_to_all x1 -> x0, starting transfers between devices: 11.9 us -> none  [per_device(): lax.all_to_all(pack(slot_index, child_tiles, head), both, split_axis=0, c...]
  transfers between devices with their start and end apart: 6 -> 5, of which waited for: 4 -> 2; matrix products, arithmetic and copies ran while one was open for 5% -> 5% of each run, Pallas kernels for 28% -> 28%
where the time goes in v6:
time: 336 us; the launch traced here: 331 us
  Pallas kernels  145 us (43%)
  blocking collectives  118 us (35%)
  waiting for transfers between devices  23.7 us (7%)
  local copies, waits for them, and re-layouts  16.9 us (5%)
  between operations  13.6 us (4%)
  starting transfers between devices  7.98 us (2%)
  other arithmetic  5.85 us (2%)
    all_to_all x1, blocking collectives, per_device(): lax.all_to_all(packed, both, split_axis=0, concat_axis=0, tiled=True)  118 us
    pallas_call x1, Pallas kernels, factor_corner(): pl.pallas_call(functools.partial(factor_kernel, 0, pairs), out_shape=(jax...  79.4 us
    pallas_call x1, Pallas kernels, finish(): pl.pallas_call(finish_kernel, grid=(steps,), out_shape=jax.ShapeDtypeStru...  51.4 us
    ppermute x2, waiting for transfers between devices, per_device(): received.append(lax.ppermute(outgoing, both, pairs))  23.6 us
    pallas_call x1, Pallas kernels, extend(): pl.pallas_call(extend_kernel, out_shape=(jax.ShapeDtypeStruct(front.shape...  11.7 us
    unnamed x8, local copies, waits for them, and re-layouts  11.6 us
  transfers between devices with their start and end apart: 5, of which 2 were waited for; matrix products, arithmetic and copies ran while one was open for 5% of the time, Pallas kernels for 28%

profile of v6, /device:TPU:1, one launch (start us, length us, event | category | flops | bytes accessed | tf_op | source)
XLA Modules:
  0.0 330.7 jit_solution(608272067635350803)
XLA Ops:
  6.5 1.1 slice.20
  7.7 0.6 copy.21
  8.3 0.0 all-gather.4.cloned.1.call-start
  8.3 0.8 fusion.12
  9.1 0.1 fusion.2
  9.2 0.2 reduce_window_sum.11
  9.4 0.2 select_reduce_fusion
  9.6 0.8 fusion.9
  10.3 0.8 multiply_add_fusion
  11.1 1.0 scatter_custom_fusion
  12.1 0.2 reshape.43
  12.3 5.5 %copy.25 = bf16[256,8,8,128]{3,1,2,0:T(8,128)(2,1)} copy(bf16[256,8,8,128]{3,2,1,0:T(8,128)(2,1)} %bitcast.74) | data formatting | bytes 8388608
  17.8 0.1 pad.4.head_ref
  17.9 2.5 pack_tiles.1
  20.3 117.8 %all_to_all.10.arrived_ref = bf16[128,272,128]{2,1,0:T(8,128)(2,1)S(1)} all-to-all(bf16[128,272,128]{2,1,0:T(8,128)(2,1)S(1)} %pack_tiles.1), channel_id=1, replica_groups=mesh['row'=8,'col'=16] {'row','col'}, dimensions={0} | all-to-all | bytes 17825792 | tf_op jit(solution)/shard_map/all_to_all | solution.py:473
  138.2 3.6 %copy-done.2 = bf16[128,272,128]{2,1,0:T(8,128)(2,1)} copy-done((bf16[128,272,128]{2,1,0:T(8,128)(2,1)}, bf16[128,272,128]{2,1,0:T(8,128)(2,1)S(1)}, u32[]{:S(2)}) %copy-start.2) | copy-done | bytes 8912920
  141.8 0.2 fusion.1
  142.0 0.1 reshape.33.id_ref
  142.1 11.7 %extend_add.1 = (bf16[2048,1024]{1,0:T(8,128)(2,1)S(1)}, bf16[1792,128]{1,0:T(8,128)(2,1)}) custom-call(s32[256]{0:T(256)S(1)} %reshape.33.id_ref, bf16[2048,1024]{1,0:T(8,128)(2,1)} %bitcast.73, bf16[128,272,128]{2,1,0:T(8,128)(2,1)} %copy-done.2), custom_call_target="tpu_custom_call" | custom-call | flops 10000000 | bytes 30000000 | tf_op jit(solution)/shard_map/extend_add/pallas_call | solution.py:322
  153.8 2.0 copy-done.1
  155.8 1.1 select_bitcast_fusion.2
  156.9 0.8 collective-permute-start.1
  157.7 1.1 fusion
  158.7 2.4 collective-permute-start
  161.2 0.7 pad_add_fusion.place_ref
  161.9 20.6 %collective-permute-done.1 = bf16[7,128,128]{2,1,0:T(8,128)(2,1)S(1)} collective-permute-done((bf16[7,128,128]{2,1,0:T(8,128)(2,1)S(1)}, bf16[7,128,128]{2,1,0:T(8,128)(2,1)S(1)}, u32[]{:S(2)}, u32[]{:S(2)}) %collective-permute-start.1) | collective-permute-done | bytes 229408 | tf_op jit(solution)/shard_map/ppermute | solution.py:490
  182.4 3.0 collective-permute-done
  185.6 2.7 broadcast_in_dim.10
  188.3 4.7 %all-to-all-start.1 = ((bf16[8,2,7,128,128]{4,3,2,1,0:T(8,128)(2,1)}), bf16[8,2,7,128,128]{4,3,2,1,0:T(8,128)(2,1)}, u32[]{:S(2)}, u32[]{:S(2)}) async-start(bf16[8,2,7,128,128]{4,3,2,1,0:T(8,128)(2,1)} %broadcast_in_dim.10), calls=%async_computation.1 | async-start | bytes 7340032 | tf_op jit(solution)/shard_map/all_to_all | solution.py:496
  193.0 79.4 %factor_corner.1 = (bf16[2,128,128]{2,1,0:T(8,128)(2,1)}, bf16[2048,2048]{1,0:T(8,128)(2,1)}, bf16[2048,2048]{1,0:T(8,128)(2,1)}) custom-call(s32[2]{0:T(128)} %pad_add_fusion.place_ref, s32[256]{0:T(256)} %constant.100.clone.unit_ref, bf16[128,2,128,128]{3,2,1,0:T(8,128)(2,1)} %bitcast.75), custom_call_target="tpu_custom_call" | custom-call | flops 89999998976 | bytes 24000000 | tf_op jit(solution)/shard_map/factor_corner/pallas_call | solution.py:248
  272.4 0.0 all-gather.4.cloned.1.call-done.row_ref
  272.5 51.4 %solve_update.1 = f32[16384,128]{1,0:T(8,128)} custom-call(s32[2]{0:T(128)} %pad_add_fusion.place_ref, bf16[2048,2048]{1,0:T(8,128)(2,1)} %get-tuple-element.18.xh_ref, bf16[2048,2048]{1,0:T(8,128)(2,1)} %get-tuple-element.19.xl_ref, bf16[16,14,128,128]{3,2,1,0:T(8,128)(2,1)} %all-gather.4.cloned.1.call-done.row_ref, ...), custom_call_target="tpu_custom_call" | custom-call | flops 40000000000 | bytes 50000000 | tf_op jit(solution)/shard_map/solve_update/pallas_call | solution.py:422
  (12 shorter events, 0.2 us)
Async XLA Ops:
  6.5 179.0 %all-gather.6.cloned.1.call-start = ((), (), s32[]{:S(2)}) async-start(), calls=%async_computation.3 | async-start | bytes 8454144 | tf_op jit(solution)/shard_map/all_gather | solution.py:460
  8.3 264.1 %all-gather.4.cloned.1.call-start = ((), (), s32[]{:S(2)}) async-start(), calls=%async_computation.2 | async-start | bytes 7798784 | tf_op jit(solution)/shard_map/all_gather | solution.py:478
  12.3 5.6 %copy-start = (bf16[128,128,128]{2,1,0:T(8,128)(2,1)S(1)}, bf16[128,128,128]{2,1,0:T(8,128)(2,1)}, u32[]{:S(2)}) copy-start(bf16[128,128,128]{2,1,0:T(8,128)(2,1)} %child_ref.1) | copy-start | bytes 12582916
  138.2 3.6 %copy-start.2 = (bf16[128,272,128]{2,1,0:T(8,128)(2,1)}, bf16[128,272,128]{2,1,0:T(8,128)(2,1)S(1)}, u32[]{:S(2)}) copy-start(bf16[128,272,128]{2,1,0:T(8,128)(2,1)S(1)} %all_to_all.10.arrived_ref) | copy-start | bytes 26738692
  153.8 2.0 copy-start.1
  156.9 25.5 %collective-permute-start.1 = (bf16[7,128,128]{2,1,0:T(8,128)(2,1)S(1)}, bf16[7,128,128]{2,1,0:T(8,128)(2,1)S(1)}, u32[]{:S(2)}, u32[]{:S(2)}) collective-permute-start(bf16[7,128,128]{2,1,0:T(8,128)(2,1)S(1)} %select_bitcast_fusion.2), channel_id=1, source_target_pairs={{0,8},{1,0},{2,24},{3,16},{4,40},{5,32},{6,56},{7,48},{8,72},{9,64... | collective-permute-start | bytes 688136 | tf_op jit(solution)/shard_map/ppermute | solution.py:490
  158.7 26.7 %collective-permute-start = (bf16[7,128,128]{2,1,0:T(8,128)(2,1)S(1)}, bf16[7,128,128]{2,1,0:T(8,128)(2,1)S(1)}, u32[]{:S(2)}, u32[]{:S(2)}) collective-permute-start(bf16[7,128,128]{2,1,0:T(8,128)(2,1)S(1)} %fusion), channel_id=1, source_target_pairs={{0,0},{1,8},{2,16},{3,24},{4,32},{5,40},{6,48},{7,56},{8,64},{9,72... | collective-permute-start | bytes 688136 | tf_op jit(solution)/shard_map/ppermute | solution.py:490
  188.3 84.1 %all-to-all-start.1 = ((bf16[8,2,7,128,128]{4,3,2,1,0:T(8,128)(2,1)}), bf16[8,2,7,128,128]{4,3,2,1,0:T(8,128)(2,1)}, u32[]{:S(2)}, u32[]{:S(2)}) async-start(bf16[8,2,7,128,128]{4,3,2,1,0:T(8,128)(2,1)} %broadcast_in_dim.10), calls=%async_computation.1 | async-start | bytes 7340032 | tf_op jit(solution)/shard_map/all_to_all | solution.py:496
Sparse Core Ops, SparseCore 0:
  10.3 143.0 all-gather.5
  155.9 79.8 all-gather.3
